TPU v7x, 512 devices: a whole 4x4x16 slice. The times are simulated.
512 devices in a mesh: dp: 8 (over y, z_hi), expert: 64 (over x, z_lo, core).
Axes of the slice: x: 4, y: 4, z: 16 (z_hi: 2, z_lo: 8; z = z_hi * 8 + z_lo), core: 2. Of those that a mesh axis runs over, the one named last changes fastest.
Arguments:
- tokens: bfloat16 [2048, 3584], P('expert'), may hold values from -6 to 6
- expert_ids: int32 [2048, 8], P('expert'), may hold values from 0 to 63, all different within a row
- router_gates: float32 [2048, 8], P('expert'), may hold values from 0.1 to 0.6
- replica_plan: int32 [64], replicated, may hold values from 0 to 63, each once
- w_gate: bfloat16 [64, 3584, 1024], P('expert', None, 'dp'), may hold values from -0.09375 to 0.09375
- w_up: bfloat16 [64, 3584, 1024], P('expert', None, 'dp'), may hold values from -0.09375 to 0.09375
- w_down: bfloat16 [64, 3584, 1024], P('expert', None, 'dp'), may hold values from -0.1875 to 0.1875
Outputs:
- mixed: bfloat16 [2048, 3584], P('expert', 'dp')
- expert_load: float32 [64], P('expert')
Inputs may be any that keep to these rules, and one draw needn't show every extreme that they name: `expert_ids`: each token names 8 different experts. `replica_plan`: each expert is named exactly once.
All inputs are finite; a program needn't handle non-finite values.
Results may differ from a plain program's by a relative error of at most 0.018.
Values may be sent and summed in bfloat16 or wider, within the bound.
A program may use at most 64 MiB of HBM per device.

v0:
```python
import jax
import jax.numpy as jnp
from jax import lax
from jax.sharding import PartitionSpec as P


def expert_part(row_block, gate_matrix, up_matrix, down_matrix):
    gate_out = jnp.dot(row_block, gate_matrix, preferred_element_type=jnp.float32)
    up_out = jnp.dot(row_block, up_matrix, preferred_element_type=jnp.float32)
    hidden = (jax.nn.silu(gate_out) * up_out).astype(jnp.bfloat16)
    return lax.dot_general(
        hidden, down_matrix, (((1,), (1,)), ((), ())), preferred_element_type=jnp.float32
    )


def per_device(tokens, expert_ids, router_gates, replica_plan, w_gate, w_up, w_down):
    tok_rows, model_width = tokens.shape
    top_k = expert_ids.shape[1]
    experts = replica_plan.shape[0]
    capacity = tok_rows // 8
    slot_total = experts * 2 * capacity
    parity = (jnp.arange(tok_rows, dtype=jnp.int32) % 2)[:, None]
    slot_keys = (expert_ids * 2 + parity).reshape(-1)
    one_hot = (slot_keys[:, None] == jnp.arange(2 * experts, dtype=jnp.int32)[None, :]).astype(
        jnp.int32
    )
    slot_pos = jnp.sum(jnp.cumsum(one_hot, axis=0) * one_hot, axis=1) - 1
    kept_mask = slot_pos < capacity
    slot_index = jnp.where(kept_mask, slot_keys * capacity + slot_pos, -1)
    selector = slot_index[:, None] == jnp.arange(slot_total, dtype=jnp.int32)[None, :]
    picker = jnp.sum(
        selector.reshape(tok_rows, top_k, slot_total).astype(jnp.bfloat16),
        axis=1,
        dtype=jnp.bfloat16,
    )
    buffer = lax.dot_general(
        picker, tokens, (((0,), (0,)), ((), ())), preferred_element_type=jnp.float32
    )
    buffer = buffer.astype(jnp.bfloat16).reshape(experts, 2, capacity, model_width)
    kept_counts = jnp.sum(one_hot * kept_mask[:, None].astype(jnp.int32), axis=0).astype(
        jnp.float32
    )
    all_counts = lax.psum(kept_counts, "expert").reshape(experts, 2)
    load_all = (all_counts[:, 0] + jnp.take(all_counts[:, 1], replica_plan, axis=0)) / (
        experts * capacity
    )
    expert_load = lax.dynamic_slice_in_dim(load_all, lax.axis_index("expert"), 1, 0)
    split_parts = (
        lax.all_to_all(w_gate, "expert", split_axis=1, concat_axis=0, tiled=True),
        lax.all_to_all(w_up, "expert", split_axis=1, concat_axis=0, tiled=True),
        lax.all_to_all(w_down, "expert", split_axis=1, concat_axis=0, tiled=True),
    )
    chosen = (
        jnp.take(split_parts[0], replica_plan, axis=0),
        jnp.take(split_parts[1], replica_plan, axis=0),
        jnp.take(split_parts[2], replica_plan, axis=0),
    )
    spare_gate, spare_up, spare_down = (
        lax.all_to_all(chosen[0], "expert", split_axis=0, concat_axis=1, tiled=True),
        lax.all_to_all(chosen[1], "expert", split_axis=0, concat_axis=1, tiled=True),
        lax.all_to_all(chosen[2], "expert", split_axis=0, concat_axis=1, tiled=True),
    )
    sendbuf = jnp.concatenate(
        [buffer[:, 0:1], jnp.take(buffer[:, 1:2], replica_plan, axis=0)], axis=1
    )
    arrived = lax.all_to_all(sendbuf, "expert", split_axis=0, concat_axis=0, tiled=True)
    sources = arrived.shape[0]
    first_half = expert_part(arrived[:, 0].reshape(-1, model_width), w_gate[0], w_up[0], w_down[0])
    second_half = expert_part(
        arrived[:, 1].reshape(-1, model_width), spare_gate[0], spare_up[0], spare_down[0]
    )
    partial_value = jnp.stack(
        [
            first_half.reshape(sources, capacity, model_width),
            second_half.reshape(sources, capacity, model_width),
        ],
        axis=1,
    )
    scattered = lax.psum_scatter(
        partial_value.astype(jnp.bfloat16), "dp", scatter_dimension=3, tiled=True
    )
    returned = lax.all_to_all(scattered, "expert", split_axis=0, concat_axis=0, tiled=True)
    holder = (
        jnp.zeros((experts,), jnp.int32).at[replica_plan].set(jnp.arange(experts, dtype=jnp.int32))
    )
    returned = jnp.concatenate(
        [returned[:, 0:1], jnp.take(returned[:, 1:2], holder, axis=0)], axis=1
    )
    weighting = router_gates.reshape(-1) * kept_mask.astype(jnp.float32)
    flat_out = returned.reshape(slot_total, -1)
    fetched = jnp.take(flat_out, jnp.maximum(slot_index, 0), axis=0).astype(jnp.float32)
    weighted = weighting[:, None] * fetched
    mixed = jnp.sum(weighted.reshape(tok_rows, top_k, -1), axis=1)
    return (mixed.astype(jnp.bfloat16), expert_load)


def solution(mesh):
    placed = (
        P("expert", None),
        P("expert", None),
        P("expert", None),
        P(),
        P("expert", None, "dp"),
        P("expert", None, "dp"),
        P("expert", None, "dp"),
    )
    return jax.shard_map(
        per_device,
        mesh=mesh,
        in_specs=placed,
        out_specs=(P("expert", "dp"), P("expert")),
        check_vma=False,
    )
```

profile of v0, /device:TPU:6, one launch (start us, length us, event | category | flops | bytes accessed | tf_op | source)
XLA Modules:
  0.0 1227.2 jit_solution(9389950563338132810)
XLA Ops:
  7.2 8.6 copy.81
  16.3 19.7 %reduce.4 = bf16[3584,128]{1,0:T(8,128)(2,1)S(1)} reduce(bf16[3584,1,128]{2,1,0:T(2,128)(2,1)S(1)} %bitcast.79, bf16[]{:T(256)} %broadcast.255), dimensions={1}, to_apply=%bitcast.73.reduce_sub_computation | reduce | bytes 1835010
  37.1 17.2 %all-to-all-start.1 = ((bf16[64,2,3584]{2,1,0:T(2,128)(2,1)}), bf16[64,2,3584]{2,1,0:T(2,128)(2,1)}, u32[]{:S(2)}, u32[]{:S(2)}) async-start(bf16[64,2,3584]{2,1,0:T(2,128)(2,1)} %reshape.285), calls=%async_computation.1 | async-start | bytes 1835008 | tf_op jit(solution)/shard_map/all_to_all | solution.py:49
  54.4 14.7 %copy.80 = bf16[1,3584,128]{2,0,1:T(2,128)(2,1)S(1)} copy(bf16[1,3584,128]{2,1,0:T(8,128)(2,1)S(1)} %copy-done.8) | data formatting | bytes 1835008 | tf_op args[5]
  69.1 19.7 %reduce.6 = bf16[3584,128]{1,0:T(8,128)(2,1)S(1)} reduce(bf16[3584,1,128]{2,1,0:T(2,128)(2,1)S(1)} %bitcast.84, bf16[]{:T(256)} %broadcast.255), dimensions={1}, to_apply=%bitcast.72.reduce_sub_computation | reduce | bytes 1835010
  89.9 9.3 all-to-all-done.1
  99.3 8.9 all-to-all-start.3
  108.1 14.7 %copy.79 = bf16[1,3584,128]{2,0,1:T(2,128)(2,1)S(1)} copy(bf16[1,3584,128]{2,1,0:T(8,128)(2,1)S(1)} %copy-done.4) | data formatting | bytes 1835008 | tf_op args[6]
  122.8 19.7 %reduce.5 = bf16[3584,128]{1,0:T(8,128)(2,1)S(1)} reduce(bf16[3584,1,128]{2,1,0:T(2,128)(2,1)S(1)} %bitcast.80, bf16[]{:T(256)} %broadcast.255), dimensions={1}, to_apply=%bitcast.71.reduce_sub_computation | reduce | bytes 1835010
  143.7 9.5 all-to-all-done.3
  153.2 9.0 all-to-all-start.5
  163.5 394.0 %psum.7 = f32[64,2]{1,0:T(8,128)S(1)} all-reduce(f32[64,2]{1,0:T(8,128)S(1)} %reshape.191), channel_id=1, replica_groups=mesh['dp'=8,'expert'=64] {'expert'}, use_global_device_ids=true, to_apply=%region_8.10 | all-reduce | flops 128 | bytes 1024 | tf_op jit(solution)/shard_map/psum | solution.py:43
  582.4 87.6 %all_to_all.73 = bf16[64,56,128]{2,1,0:T(8,128)(2,1)S(1)} all-to-all(bf16[64,56,128]{2,1,0:T(8,128)(2,1)S(1)} %get-tuple-element.17), channel_id=1, replica_groups=mesh['dp'=8,'expert'=64] {'expert'}, dimensions={0} | all-to-all | bytes 1835008 | tf_op jit(solution)/shard_map/all_to_all | solution.py:59
  670.0 8.9 all-to-all-start.4
  682.2 7.0 reshape.187
  705.2 18.7 %all-to-all-done.4 = bf16[64,56,128]{2,1,0:T(8,128)(2,1)} async-done(((bf16[64,56,128]{2,1,0:T(8,128)(2,1)}), bf16[64,56,128]{2,1,0:T(8,128)(2,1)}, u32[]{:S(2)}, u32[]{:S(2)}) %all-to-all-start.4) | async-done | bytes 917536 | tf_op jit(solution)/shard_map/all_to_all | solution.py:60
  724.0 171.3 %all_to_all.74 = bf16[64,2,4,3584]{3,2,1,0:T(4,128)(2,1)} all-to-all(bf16[64,2,4,3584]{3,2,1,0:T(4,128)(2,1)} %pad_maximum_fusion), channel_id=1, replica_groups=mesh['dp'=8,'expert'=64] {'expert'}, dimensions={0} | all-to-all | bytes 7340032 | tf_op jit(solution)/shard_map/all_to_all | solution.py:66
  895.2 9.5 all-to-all-start.6
  922.2 27.6 %all-to-all-done.6 = bf16[64,56,128]{2,1,0:T(8,128)(2,1)} async-done(((bf16[64,56,128]{2,1,0:T(8,128)(2,1)}), bf16[64,56,128]{2,1,0:T(8,128)(2,1)}, u32[]{:S(2)}, u32[]{:S(2)}) %all-to-all-start.6) | async-done | bytes 917536 | tf_op jit(solution)/shard_map/all_to_all | solution.py:61
  953.9 11.4 copy.64
  965.2 12.3 %reshape.275 = bf16[3584,512]{1,0:T(8,128)(2,1)} reshape(bf16[3584,2,4,64]{3,2,1,0:T(4,128)(2,1)} %bitcast.78) | data formatting | bytes 7340032
  977.6 200.1 %reduce-scatter.4.cloned.1.call-done = bf16[448,512]{1,0:T(8,128)(2,1)} async-done(((bf16[3584,512]{1,0:T(8,128)(2,1)}), bf16[448,512]{1,0:T(8,128)(2,1)}) %reduce-scatter.4.cloned.1.call-update) | async-done | bytes 458768
  1181.4 5.9 all-to-all-start.7
  1189.2 26.6 %all-to-all-done.7 = bf16[64,2,4,448]{3,2,1,0:T(4,128)(2,1)S(1)} async-done(((bf16[64,2,4,448]{3,2,1,0:T(4,128)(2,1)}), bf16[64,2,4,448]{3,2,1,0:T(4,128)(2,1)S(1)}, u32[]{:S(2)}, u32[]{:S(2)}) %all-to-all-start.7) | async-done | bytes 458784 | tf_op jit(solution)/shard_map/all_to_all | solution.py:82
  (106 shorter events, 80.5 us)
Async XLA Ops:
  7.2 672.1 %copy-start = (bf16[32,3584]{1,0:T(8,128)(2,1)S(1)}, bf16[32,3584]{1,0:T(8,128)(2,1)}, u32[]{:S(2)}) copy-start(bf16[32,3584]{1,0:T(8,128)(2,1)} %param.9) | copy-start | bytes 688132
  37.1 17.2 %copy-start.8 = (bf16[1,3584,128]{2,1,0:T(8,128)(2,1)S(1)}, bf16[1,3584,128]{2,1,0:T(8,128)(2,1)}, u32[]{:S(2)}) copy-start(bf16[1,3584,128]{2,1,0:T(8,128)(2,1)} %param.14) | copy-start | bytes 2752516
  37.1 62.1 %all-to-all-start.1 = ((bf16[64,2,3584]{2,1,0:T(2,128)(2,1)}), bf16[64,2,3584]{2,1,0:T(2,128)(2,1)}, u32[]{:S(2)}, u32[]{:S(2)}) async-start(bf16[64,2,3584]{2,1,0:T(2,128)(2,1)} %reshape.285), calls=%async_computation.1 | async-start | bytes 1835008 | tf_op jit(solution)/shard_map/all_to_all | solution.py:49
  89.9 18.2 %copy-start.4 = (bf16[1,3584,128]{2,1,0:T(8,128)(2,1)S(1)}, bf16[1,3584,128]{2,1,0:T(8,128)(2,1)}, u32[]{:S(2)}) copy-start(bf16[1,3584,128]{2,1,0:T(8,128)(2,1)} %param.15) | copy-start | bytes 2752516
  99.3 53.9 %all-to-all-start.3 = ((bf16[64,2,3584]{2,1,0:T(2,128)(2,1)}), bf16[64,2,3584]{2,1,0:T(2,128)(2,1)}, u32[]{:S(2)}, u32[]{:S(2)}) async-start(bf16[64,2,3584]{2,1,0:T(2,128)(2,1)} %reshape.283), calls=%async_computation.3 | async-start | bytes 1835008 | tf_op jit(solution)/shard_map/all_to_all | solution.py:50
  142.5 19.7 %copy-start.10 = (s32[32,8]{0,1:T(8,128)S(1)}, s32[32,8]{0,1:T(8,128)}, u32[]{:S(2)}) copy-start(s32[32,8]{0,1:T(8,128)} %param.10) | copy-start | bytes 3076
  143.7 413.8 %copy-start.12 = (s32[64]{0:T(128)S(1)}, s32[64]{0:T(128)}, u32[]{:S(2)}) copy-start(s32[64]{0:T(128)} %param.12) | copy-start | bytes 772
  153.2 423.8 %all-to-all-start.5 = ((bf16[64,2,3584]{2,1,0:T(2,128)(2,1)}), bf16[64,2,3584]{2,1,0:T(2,128)(2,1)S(1)}, u32[]{:S(2)}, u32[]{:S(2)}) async-start(bf16[64,2,3584]{2,1,0:T(2,128)(2,1)} %reshape.281), calls=%async_computation.5 | async-start | bytes 1835008 | tf_op jit(solution)/shard_map/all_to_all | solution.py:51
  577.8 3.1 copy-start.6
  578.8 2.0 copy-start.7
  670.0 53.9 %all-to-all-start.4 = ((bf16[64,56,128]{2,1,0:T(8,128)(2,1)}), bf16[64,56,128]{2,1,0:T(8,128)(2,1)}, u32[]{:S(2)}, u32[]{:S(2)}) async-start(bf16[64,56,128]{2,1,0:T(8,128)(2,1)} %get-tuple-element.19), calls=%async_computation.4 | async-start | bytes 1835008 | tf_op jit(solution)/shard_map/all_to_all | solution.py:60
  895.2 54.6 %all-to-all-start.6 = ((bf16[64,56,128]{2,1,0:T(8,128)(2,1)}), bf16[64,56,128]{2,1,0:T(8,128)(2,1)}, u32[]{:S(2)}, u32[]{:S(2)}) async-start(bf16[64,56,128]{2,1,0:T(8,128)(2,1)} %get-tuple-element.18), calls=%async_computation.6 | async-start | bytes 1835008 | tf_op jit(solution)/shard_map/all_to_all | solution.py:61
  904.7 272.9 %reduce-scatter.4.cloned.1.call-start = ((), (), s32[]{:S(2)}) async-start(), calls=%async_computation.9 | async-start | bytes 4128768
  915.0 2.5 copy-start.3
  915.0 2.6 copy-start.9
  917.5 1.2 copy-start.5
  918.2 1.6 copy-start.2
  977.6 210.9 %copy-start.11 = (f32[32,8]{0,1:T(8,128)S(1)}, f32[32,8]{0,1:T(8,128)}, u32[]{:S(2)}) copy-start(f32[32,8]{0,1:T(8,128)} %param.11) | copy-start | bytes 3076
  1181.4 34.4 %all-to-all-start.7 = ((bf16[64,2,4,448]{3,2,1,0:T(4,128)(2,1)}), bf16[64,2,4,448]{3,2,1,0:T(4,128)(2,1)S(1)}, u32[]{:S(2)}, u32[]{:S(2)}) async-start(bf16[64,2,4,448]{3,2,1,0:T(4,128)(2,1)} %copy.60), calls=%async_computation.7 | async-start | bytes 1048576 | tf_op jit(solution)/shard_map/all_to_all | solution.py:82
  1217.4 2.5 copy-start.1
Sparse Core Ops, SparseCore 0:
  977.7 199.9 reduce-scatter.3
where the time goes:
time: 1240 us; the launch traced here: 1230 us
  blocking collectives  653 us (53%)
  waiting for transfers between devices  292 us (24%)
  local copies, waits for them, and re-layouts  125 us (10%)
  other arithmetic  71.9 us (6%)
  starting transfers between devices  59.6 us (5%)
  between operations  14.9 us (1%)
    psum x1, blocking collectives, per_device(): all_counts = lax.psum(kept_counts, 'expert').reshape(experts, 2)  394 us
    unnamed x2, waiting for transfers between devices  200 us
    all_to_all x1, blocking collectives, per_device(): lax.all_to_all(sendbuf, 'expert', split_axis=0, concat_axis=0, tiled=True)  171 us
    all_to_all x1, blocking collectives, per_device(): lax.all_to_all(chosen[0], 'expert', split_axis=0, concat_axis=1, tiled=True)  87.6 us
    unnamed x46, local copies, waits for them, and re-layouts  83.7 us
    unnamed x3, other arithmetic  59 us
    all_to_all x1, waiting for transfers between devices, per_device(): lax.all_to_all(chosen[2], 'expert', split_axis=0, concat_axis=1, tiled=True)  27.6 us
    all_to_all x1, waiting for transfers between devices, per_device(): lax.all_to_all(scattered, 'expert', split_axis=0, concat_axis=0, tiled=True)  26.6 us
  transfers between devices with their start and end apart: 7, of which 6 were waited for; matrix products, arithmetic and copies ran while one was open for 11% of the time, Pallas kernels for 0%

commit v1 on v0

v1 whole, which is shorter than its diff:
```python
import jax
import jax.numpy as jnp
from jax import lax
from jax.sharding import PartitionSpec as P


def per_device(tokens, expert_ids, router_gates, replica_plan, w_gate, w_up, w_down):
    tok_rows, top_k = expert_ids.shape
    experts = replica_plan.shape[0]
    capacity = tok_rows // 8
    mine = lax.axis_index("expert")
    ids_all = lax.all_gather(expert_ids, "expert", tiled=True)
    gates_all = lax.all_gather(router_gates, "expert", tiled=True)
    rows_all = lax.all_gather(tokens, "expert", tiled=True)

    def kept_of(expert):
        hit = jnp.any(ids_all == expert, axis=1).reshape(-1, tok_rows // 2, 2)
        before = jnp.cumsum(hit.astype(jnp.int32), axis=1)
        return hit & (before <= capacity)

    own = kept_of(mine)
    copied = kept_of(replica_plan[mine])
    load = (
        jnp.sum(own[:, :, 0].astype(jnp.float32)) + jnp.sum(copied[:, :, 1].astype(jnp.float32))
    ) / (experts * capacity)
    weight = jnp.sum(jnp.where(ids_all == mine, gates_all, 0.0), axis=1) * own.reshape(-1).astype(
        jnp.float32
    )
    gate_out = jnp.dot(rows_all, w_gate[0], preferred_element_type=jnp.float32)
    up_out = jnp.dot(rows_all, w_up[0], preferred_element_type=jnp.float32)
    hidden = (jax.nn.silu(gate_out) * up_out * weight[:, None]).astype(jnp.bfloat16)
    hidden_all = lax.all_gather(hidden, "dp", axis=1, tiled=True)
    down = lax.all_to_all(w_down[0], "dp", split_axis=0, concat_axis=1, tiled=True)
    partial_value = lax.dot_general(
        hidden_all, down, (((1,), (1,)), ((), ())), preferred_element_type=jnp.float32
    ).astype(jnp.bfloat16)
    mixed = lax.psum_scatter(partial_value, "expert", scatter_dimension=0, tiled=True)
    return mixed, load.reshape(1)


def solution(mesh):
    placed = (
        P("expert", None),
        P("expert", None),
        P("expert", None),
        P(),
        P("expert", None, "dp"),
        P("expert", None, "dp"),
        P("expert", None, "dp"),
    )
    return jax.shard_map(
        per_device,
        mesh=mesh,
        in_specs=placed,
        out_specs=(P("expert", "dp"), P("expert")),
        check_vma=False,
    )
```

time: 1240 us -> 913 us (0.74)
  the two profiles are of different devices: /device:TPU:6 before, /device:TPU:8 now
where the time goes in v1:
time: 913 us
  waiting for transfers between devices  581 us (64%)
  blocking collectives  289 us (32%)
  matrix products  19.4 us (2%)
  between operations  16.4 us (2%)
    reduce_scatter x1, waiting for transfers between devices, per_device(): lax.psum_scatter(partial_value, 'expert', scatter_dimension=0, tiled=True)  427 us
    all_gather x1, waiting for transfers between devices, per_device(): hidden_all = lax.all_gather(hidden, 'dp', axis=1, tiled=True)  153 us
    all_gather x1, blocking collectives, per_device(): ids_all = lax.all_gather(expert_ids, 'expert', tiled=True)  128 us
    all_gather x1, blocking collectives, per_device(): gates_all = lax.all_gather(router_gates, 'expert', tiled=True)  114 us
    all_to_all x1, blocking collectives, per_device(): lax.all_to_all(w_down[0], 'dp', split_axis=0, concat_axis=1, tiled=True)  46.3 us
  transfers between devices with their start and end apart: 3, of which 2 were waited for; matrix products, arithmetic and copies ran while one was open for 1% of the time, Pallas kernels for 0%

profile of v1, /device:TPU:8, one launch (start us, length us, event | category | flops | bytes accessed | tf_op | source)
XLA Modules:
  0.0 913.0 jit_solution(10194597790695269862)
XLA Ops:
  7.2 0.7 all-gather.5.cloned.1.call-update
  8.0 1.2 dynamic_slice.3
  9.2 128.5 %all-gather = s32[64,32,8]{1,2,0:T(8,128)S(1)} all-gather(s32[1,32,8]{1,2,0:T(8,128)} %bitcast.31), channel_id=1, replica_groups=mesh['dp'=8,'expert'=64] {'expert'}, dimensions={0}, use_global_device_ids=true | all-gather | bytes 66560 | tf_op jit(solution)/shard_map/all_gather | solution.py:12
  137.7 0.8 fusion.8
  138.6 0.1 copy.16
  138.6 0.1 reshape.47
  138.8 0.2 copy.17
  139.0 0.1 reduce-window_compare_fusion
  139.1 0.1 copy.18
  139.2 0.3 le.15
  139.6 114.0 %all-gather.1 = f32[64,32,8]{1,2,0:T(8,128)S(1)} all-gather(f32[1,32,8]{1,2,0:T(8,128)} %bitcast.32), channel_id=1, replica_groups=mesh['dp'=8,'expert'=64] {'expert'}, dimensions={0}, use_global_device_ids=true | all-gather | bytes 66560 | tf_op jit(solution)/shard_map/all_gather | solution.py:13
  253.5 0.1 select_reduce_fusion
  253.8 8.8 fusion.5
  262.5 0.6 copy-done.2
  263.1 4.8 fusion.1
  268.0 46.3 %all_to_all.19 = bf16[8,448,128]{2,1,0:T(8,128)(2,1)S(1)} all-to-all(bf16[8,448,128]{2,1,0:T(8,128)(2,1)S(1)} %bitcast.29), channel_id=1, replica_groups=mesh['dp'=8,'expert'=64] {'dp'}, dimensions={0} | all-to-all | bytes 1835008 | tf_op jit(solution)/shard_map/all_to_all | solution.py:33
  314.3 153.4 %all-gather.7.cloned.1.call-done = bf16[2048,1024]{1,0:T(8,128)(2,1)} async-done(((bf16[2048,128]{1,0:T(8,128)(2,1)}), bf16[2048,1024]{1,0:T(8,128)(2,1)}) %all-gather.7.cloned.1.call-update) | async-done | bytes 4194320 | tf_op jit(solution)/shard_map/all_gather | solution.py:32
  467.7 5.9 convolution_convert_fusion
  473.8 0.3 copy.24
  474.1 0.2 copy.22
  474.3 0.3 copy.25
  474.7 1.1 fusion.9
  475.7 1.0 convert_reduce_fusion
  478.1 427.3 %reduce-scatter.2.cloned.1.call-done = bf16[32,448]{1,0:T(8,128)(2,1)} async-done(((bf16[2048,448]{1,0:T(8,128)(2,1)}), bf16[32,448]{1,0:T(8,128)(2,1)}) %reduce-scatter.2.cloned.1.call-update) | async-done | bytes 28688 | tf_op jit(solution)/shard_map/reduce_scatter | solution.py:37
  (21 shorter events, 0.4 us)
Async XLA Ops:
  7.2 246.6 %copy-start = (bf16[1,3584,128]{2,1,0:T(8,128)(2,1)S(1)}, bf16[1,3584,128]{2,1,0:T(8,128)(2,1)}, u32[]{:S(2)}) copy-start(bf16[1,3584,128]{2,1,0:T(8,128)(2,1)} %param.11) | copy-start | bytes 2752516
  7.2 255.4 %copy-start.3 = (bf16[1,3584,128]{2,1,0:T(8,128)(2,1)S(1)}, bf16[1,3584,128]{2,1,0:T(8,128)(2,1)}, u32[]{:S(2)}) copy-start(bf16[1,3584,128]{2,1,0:T(8,128)(2,1)} %param.12) | copy-start | bytes 2752516
  7.2 246.5 %all-gather.5.cloned.1.call-start = ((), (), s32[]{:S(2)}) async-start(), calls=%async_computation.2 | async-start | bytes 14909440 | tf_op jit(solution)/shard_map/all_gather | solution.py:14
  7.9 459.8 %all-gather.7.cloned.1.call-start = ((), (), s32[]{:S(2)}) async-start(), calls=%async_computation.3 | async-start | bytes 4718592 | tf_op jit(solution)/shard_map/all_gather | solution.py:32
  253.8 9.3 %copy-start.2 = (bf16[2048,3584]{1,0:T(8,128)(2,1)S(1)}, bf16[2048,3584]{1,0:T(8,128)(2,1)}, u32[]{:S(2)}) copy-start(bf16[2048,3584]{1,0:T(8,128)(2,1)} %all-gather.5.cloned.1.call-done) | copy-start | bytes 44040196
  263.1 4.9 copy-start.1
  267.9 637.4 %reduce-scatter.2.cloned.1.call-start = ((), (), s32[]{:S(2)}) async-start(), calls=%async_computation.4 | async-start | bytes 2129920 | tf_op jit(solution)/shard_map/reduce_scatter | solution.py:37
Sparse Core Ops, SparseCore 0:
  10.2 140.3 all-gather.4
  268.0 199.6 all-gather.6
  473.8 431.5 reduce-scatter.1

commit v2 on v1

v2 whole, which is shorter than its diff:
```python
import jax
import jax.numpy as jnp
from jax import lax
from jax.experimental import pallas as pl
from jax.experimental.pallas import tpu as pltpu
from jax.sharding import PartitionSpec as P

BF16, F32 = jnp.bfloat16, jnp.float32
ROWS, HALF = 32, 16
D = 3584
WA = 1792
WB = D - WA
EXTRA = 128
CAP = 4
SLABS = 8
QUARTER, EIGHTH, PADDED = 896, 448, 512


def kernel(
    tokens, ids, gates, plan, w_gate, w_up, w_down,
    out, load,
    buf_a, buf_b, wgu, wd, hid, part, xin1, xin2, xr, zin, zout, cnt, cnt_in,
    loc, w_s, w_r, wd_s, wd_r, wf_s, wf_r, ax_s, ax_r, az_s, az_r, bz_s, bz_r, bx_s, bx_r,
    h_s, h_r, x1_s, x1_r, x2_s, x2_r, z_s, z_r, c_s, c_r,
):
    dp = lax.axis_index("dp")
    ex = lax.axis_index("expert")
    y, zh = lax.div(dp, 2), lax.rem(dp, 2)
    x, zl, core = lax.div(ex, 16), lax.rem(lax.div(ex, 2), 8), lax.rem(ex, 2)
    z = zh * 8 + zl

    def at_x(dx):
        return (dp, ex + (lax.rem(x + dx + 4, 4) - x) * 16)

    def at_y(dy):
        return (lax.rem(y + dy, 4) * 2 + zh, ex)

    def at_z(dz):
        new = lax.rem(z + dz + 16, 16)
        return (y * 2 + lax.div(new, 8), ex + (lax.rem(new, 8) - zl) * 2)

    peer = (dp, ex + 1 - 2 * core)

    def send(src, dst, ss, rs, dev):
        pltpu.make_async_remote_copy(
            src_ref=src, dst_ref=dst, send_sem=ss, recv_sem=rs, device_id=dev,
            device_id_type=pl.DeviceIdType.MESH,
        ).start()

    def arrived(ref, sem):
        pltpu.make_async_remote_copy(
            src_ref=ref, dst_ref=ref, send_sem=sem, recv_sem=sem, device_id=peer,
            device_id_type=pl.DeviceIdType.MESH,
        ).wait_recv()

    def sent(ref, sem):
        pltpu.make_async_remote_copy(
            src_ref=ref, dst_ref=ref, send_sem=sem, recv_sem=sem, device_id=peer,
            device_id_type=pl.DeviceIdType.MESH,
        ).wait_send()

    def xs(q):
        return lax.rem(x + (0, 3, 1, 2)[q], 4)

    def label(j):
        return lax.rem(zl + (1 - 2 * lax.rem(j, 2)) * lax.div(j + 1, 2) + 8, 8)

    low, high = pl.ds(0, HALF), pl.ds(HALF, HALF)
    core_lanes = pl.multiple_of(core * 256, 128)

    own_a, own_b = buf_a.at[zl, x], buf_b.at[zl, x]
    local = [
        pltpu.make_async_copy(tokens.at[:, pl.ds(0, WA)], own_a, loc.at[0]),
        pltpu.make_async_copy(tokens.at[:, pl.ds(WA, WB)], own_b.at[:, pl.ds(0, WB)], loc.at[1]),
        pltpu.make_async_copy(w_gate.at[0], wgu.at[:, pl.ds(core_lanes, 128)], loc.at[2]),
        pltpu.make_async_copy(w_up.at[0], wgu.at[:, pl.ds(core_lanes + 128, 128)], loc.at[3]),
        pltpu.make_async_copy(
            w_down.at[y],
            wd.at[:, pl.ds(0, EIGHTH), pl.ds(pl.multiple_of((y * 2 + core) * 128, 128), 128)],
            loc.at[4],
        ),
    ]
    for copy in local:
        copy.start()

    barrier = pltpu.get_barrier_semaphore()
    partners = [at_x(1), at_x(-1), at_z(1), at_z(-1), at_y(1), at_y(2), at_y(3), peer]
    for dev in partners:
        pl.semaphore_signal(barrier, inc=1, device_id=dev, device_id_type=pl.DeviceIdType.MESH)

    expert_lane = lax.broadcasted_iota(jnp.int32, (ROWS, EXTRA), 1)
    expert_lane = jnp.where(expert_lane >= 64, expert_lane - 64, expert_lane)
    chosen = jnp.zeros((ROWS, EXTRA), F32)
    weight = jnp.zeros((ROWS, EXTRA), F32)
    for k in range(8):
        hit = ids[:, k : k + 1] == expert_lane
        chosen = chosen + jnp.where(hit, 1.0, 0.0)
        weight = weight + jnp.where(hit, gates[:, k : k + 1], 0.0)
    row = lax.broadcasted_iota(jnp.int32, (ROWS, ROWS), 0)
    col = lax.broadcasted_iota(jnp.int32, (ROWS, ROWS), 1)
    earlier = ((col < row) & (((row - col) & 1) == 0)).astype(BF16)
    before = jnp.dot(earlier, chosen.astype(BF16), preferred_element_type=F32)
    weight = jnp.where(before < CAP - 0.5, weight, 0.0)
    coarse = weight.astype(BF16)
    fine = (weight - coarse.astype(F32)).astype(BF16)
    lanes = lax.broadcasted_iota(jnp.int32, (ROWS, EXTRA), 1)
    buf_b[zl, x, :, pl.ds(WB, EXTRA)] = jnp.where(
        lanes < 64, coarse.astype(F32), fine.astype(F32)
    ).astype(BF16)
    wd[:, pl.ds(EIGHTH, PADDED - EIGHTH), :] = jnp.zeros((2, PADDED - EIGHTH, 1024), BF16)
    cnt[...] = jnp.zeros_like(cnt)
    local[0].wait()
    local[1].wait()
    pl.semaphore_wait(barrier, len(partners))

    def send_az(jd, q):
        odd = lax.rem(jd, 2) == 1
        up = odd if q < 2 else (odd & (jd != 7))
        way = jnp.where(up, 1, -1)
        ref = buf_a.at[lax.rem(zl - way * (lax.div(jd + 1, 2) - 1) + 8, 8), xs(q)]
        send(ref, ref, az_s.at[jd, q], az_r.at[jd, q], at_z(way))

    def send_bz(jd, up, rows, sem):
        way = 1 if up is True else -1 if up is False else jnp.where(up, 1, -1)
        ref = buf_b.at[lax.rem(zl - way * (lax.div(jd + 1, 2) - 1) + 8, 8), x, rows]
        send(ref, ref, bz_s.at[sem], bz_r.at[sem], at_z(way))

    def send_bx(j):
        ref = buf_b.at[label(j), x]
        send(ref, ref, bx_s.at[j, 0], bx_r.at[j, 0], at_x(1))
        send(ref, ref, bx_s.at[j, 1], bx_r.at[j, 1], at_x(-1))

    whole = pl.ds(0, ROWS)
    send_bz(jnp.int32(1), True, whole, 1)
    send_bz(jnp.int32(2), False, whole, 2)
    send(own_a, own_a, ax_s.at[0], ax_r.at[0], at_x(1))
    send(own_a, own_a, ax_s.at[1], ax_r.at[1], at_x(-1))
    send_bx(jnp.int32(0))
    send_az(jnp.int32(1), 0)
    send_az(jnp.int32(2), 0)
    for i, src in enumerate((w_gate, w_up)):
        dst = wgu.at[:, pl.ds(core_lanes + 128 * i, 128)]
        send(src.at[0], dst, w_s.at[i], w_r.at[i], peer)

    def wd_lanes(row_block, which):
        return wd.at[
            :, pl.ds(0, EIGHTH), pl.ds(pl.multiple_of((row_block * 2 + which) * 128, 128), 128)
        ]

    for k in (1, 2, 3):
        send(
            w_down.at[lax.rem(y + k, 4)], wd_lanes(y, core), wd_s.at[k], wd_r.at[k], at_y(k)
        )

    def gather(j):
        nxt = j + 1

        @pl.when(nxt <= 6)
        def _():
            arrived(buf_b.at[label(nxt), x], bz_r.at[nxt])

            @pl.when(nxt <= 4)
            def _():
                send_bz(nxt + 2, lax.rem(nxt, 2) == 1, whole, nxt + 2)

            @pl.when(nxt == 5)
            def _():
                send_bz(jnp.int32(7), True, low, 7)

            @pl.when(nxt == 6)
            def _():
                send_bz(jnp.int32(7), False, high, 8)

        @pl.when(nxt == 7)
        def _():
            arrived(buf_b.at[label(nxt), x, low], bz_r.at[7])
            arrived(buf_b.at[label(nxt), x, high], bz_r.at[8])

        @pl.when(nxt <= 7)
        def _():
            send_bx(nxt)

        @pl.when(j == 0)
        def _():
            one, two = jnp.int32(1), jnp.int32(2)
            ref = buf_a.at[zl, xs(1)]
            arrived(ref, ax_r.at[0])
            send(ref.at[low], ref.at[low], ax_s.at[2], ax_r.at[2], at_x(1))
            send_az(one, 1)
            send_az(two, 1)
            ref = buf_a.at[zl, xs(2)]
            arrived(ref, ax_r.at[1])
            send(ref.at[high], ref.at[high], ax_s.at[3], ax_r.at[3], at_x(-1))
            send_az(one, 2)
            send_az(two, 2)
            arrived(buf_a.at[zl, xs(3), low], ax_r.at[2])
            arrived(buf_a.at[zl, xs(3), high], ax_r.at[3])
            send_az(one, 3)
            send_az(two, 3)

        @pl.when(j > 0)
        def _():
            for q in range(4):
                arrived(buf_a.at[label(j), xs(q)], az_r.at[j, q])
                onward = (j <= 4) | (j == 5 if q < 2 else j == 6)

                @pl.when(onward)
                def _():
                    send_az(jnp.minimum(j + 2, 7), q)

        ref = buf_b.at[label(j), xs(1)]
        arrived(ref, bx_r.at[j, 0])
        send(ref.at[low], ref.at[low], bx_s.at[j, 2], bx_r.at[j, 2], at_x(1))
        ref = buf_b.at[label(j), xs(2)]
        arrived(ref, bx_r.at[j, 1])
        send(ref.at[high], ref.at[high], bx_s.at[j, 3], bx_r.at[j, 3], at_x(-1))
        arrived(buf_b.at[label(j), xs(3), low], bx_r.at[j, 2])
        arrived(buf_b.at[label(j), xs(3), high], bx_r.at[j, 3])

    def experts(j):
        @pl.when(j == 0)
        def _():
            local[2].wait()
            local[3].wait()
            other = pl.multiple_of((1 - core) * 256, 128)
            for i in range(2):
                arrived(wgu.at[:, pl.ds(other + 128 * i, 128)], w_r.at[i])

        slab = label(j)
        acc = jnp.dot(
            buf_a[slab].reshape(128, WA), wgu[pl.ds(0, WA), :], preferred_element_type=F32
        )
        acc = acc + jnp.dot(
            buf_b[slab, :, :, pl.ds(0, WB)].reshape(128, WB),
            wgu[pl.ds(WA, WB), :],
            preferred_element_type=F32,
        )
        mix = buf_b[slab, :, :, pl.ds(WB, EXTRA)].reshape(128, EXTRA)
        lane = lax.broadcasted_iota(jnp.int32, (EXTRA, 256), 0)
        unit = lax.broadcasted_iota(jnp.int32, (EXTRA, 256), 1)
        wanted = (ex - core) + (unit >= 128).astype(jnp.int32)
        pick = ((lane == wanted) | (lane == wanted + 64)).astype(BF16)
        scale = jnp.dot(mix, pick, preferred_element_type=F32)
        gate_out = jnp.concatenate([acc[:, 0:128], acc[:, 256:384]], axis=1)
        up_out = jnp.concatenate([acc[:, 128:256], acc[:, 384:512]], axis=1)
        hidden = gate_out / (1.0 + jnp.exp(-gate_out)) * up_out * scale
        hid[slab, y] = hidden.astype(BF16)
        for k in (1, 2, 3):
            ref = hid.at[slab, y]
            send(ref, ref, h_s.at[j, k], h_r.at[j, k], at_y(k))
        kept = jnp.where(mix.astype(F32) > 0.0, 1.0, 0.0).astype(BF16)
        r = lax.broadcasted_iota(jnp.int32, (8, 128), 0)
        t = lax.broadcasted_iota(jnp.int32, (8, 128), 1)
        parity = (r == (t & 1)).astype(BF16)
        cnt[...] += jnp.dot(parity, kept, preferred_element_type=F32)

        @pl.when(j == 0)
        def _():
            local[4].wait()
            ref = wd_lanes(y, core)
            send(ref, ref, wf_s.at[0], wf_r.at[0], peer)
            for k in (1, 2, 3):
                ref = wd_lanes(lax.rem(y - k + 4, 4), core)
                arrived(ref, wd_r.at[k])
                send(ref, ref, wf_s.at[k], wf_r.at[k], peer)

    def down(j):
        @pl.when(j == 0)
        def _():
            for k in range(4):
                arrived(wd_lanes(lax.rem(y - k + 4, 4), 1 - core), wf_r.at[k])

        slab = label(j)
        for k in (1, 2, 3):
            arrived(hid.at[slab, lax.rem(y - k + 4, 4)], h_r.at[j, k])
        joined = jnp.concatenate([hid[slab, i] for i in range(4)], axis=1)
        for side in range(2):
            value = lax.dot_general(
                joined, wd[side], (((1,), (1,)), ((), ())), preferred_element_type=F32
            )
            part[slab, side] = value.astype(BF16).reshape(4, ROWS, PADDED)
        far = part.at[slab, :, xs(3)]
        send(far.at[:, low], xin1.at[j, 0], x1_s.at[j, 0], x1_r.at[j, 0], at_x(1))
        send(far.at[:, high], xin1.at[j, 1], x1_s.at[j, 1], x1_r.at[j, 1], at_x(-1))

    def add_far(j):
        slab = label(j)
        for i, (q, rows, step) in enumerate(((2, low, 1), (1, high, -1))):
            arrived(xin1.at[j, i], x1_r.at[j, i])
            there = part[slab, :, xs(q), rows, :].astype(F32) + xin1[j, i].astype(F32)
            part[slab, :, xs(q), rows, :] = there.astype(BF16)
            send(part.at[slab, :, xs(q)], xin2.at[j, i], x2_s.at[j, i], x2_r.at[j, i], at_x(step))

    def z_step(s, way, side, first=False, second=False):
        slab = lax.rem(zl - s * way + 8, 8)
        half = lax.div(lax.rem(z + way * (8 - s) + 16, 16), 8)
        value = xr[slab, half]
        rows = low if side == 0 else high
        if first:
            zout[side, s] = value.astype(BF16)
            send(
                zout.at[side, s, rows], zin.at[side, s, rows],
                z_s.at[side, s], z_r.at[side, s], at_z(way),
            )
            return
        if second:
            arrived(zin.at[side, s - 1, rows], z_r.at[side, s - 1])
            zout[side, s] = value.astype(BF16)
            more = xr[slab, half, rows, :] + zin[side, s - 1, rows, :].astype(F32)
            zout[side, s, rows, :] = more.astype(BF16)
        else:
            arrived(zin.at[side, s - 1], z_r.at[side, s - 1])
            zout[side, s] = (value + zin[side, s - 1].astype(F32)).astype(BF16)
        send(zout.at[side, s], zin.at[side, s], z_s.at[side, s], z_r.at[side, s], at_z(way))

    def add_near(j):
        slab = label(j)
        arrived(xin2.at[j, 0], x2_r.at[j, 0])
        arrived(xin2.at[j, 1], x2_r.at[j, 1])
        xr[slab] = (
            part[slab, :, x].astype(F32) + xin2[j, 0].astype(F32) + xin2[j, 1].astype(F32)
        )

        @pl.when(j == 0)
        def _():
            z_step(0, 1, 0, first=True)
            z_step(0, -1, 1, first=True)

        @pl.when(j == 1)
        def _():
            z_step(1, 1, 0, second=True)

        @pl.when(j == 2)
        def _():
            z_step(1, -1, 1, second=True)

        @pl.when((j >= 3) & (lax.rem(j, 2) == 1))
        def _():
            z_step(lax.div(j + 1, 2), 1, 0)

        @pl.when((j >= 3) & ((lax.rem(j, 2) == 0) | (j == 7)))
        def _():
            z_step(lax.div(j + 1, 2), -1, 1)

    def turn(i, carry):
        @pl.when(i < SLABS)
        def _():
            gather(i)

        @pl.when(i >= 3)
        def _():
            add_near(i - 3)

        @pl.when((i >= 2) & (i < SLABS + 2))
        def _():
            add_far(i - 2)

        @pl.when((i >= 1) & (i < SLABS + 1))
        def _():
            down(i - 1)

        @pl.when(i < SLABS)
        def _():
            experts(i)

        @pl.when(i == SLABS)
        def _():
            send(cnt, cnt_in, c_s, c_r, peer)

        return carry

    lax.fori_loop(0, SLABS + 3, turn, 0)

    def last(s, carry):
        z_step(s, 1, 0)
        z_step(s, -1, 1)
        return carry

    lax.fori_loop(5, 8, last, 0)

    arrived(cnt_in, c_r)
    total = cnt[...] + cnt_in[...]
    r = lax.broadcasted_iota(jnp.int32, (8, 128), 0)
    t = lax.broadcasted_iota(jnp.int32, (8, 128), 1)
    copied = plan[ex]
    served = ((r == 0) & (t == ex)) | ((r == 1) & (t == copied))
    amount = jnp.sum(jnp.where(served, total, 0.0), axis=1, keepdims=True)
    amount = jnp.sum(amount, axis=0, keepdims=True) * (1.0 / 256.0)
    load[...] = jnp.broadcast_to(amount, (8, 128))

    arrived(zin.at[0, 7], z_r.at[0, 7])
    arrived(zin.at[1, 7], z_r.at[1, 7])
    mixed = xr[zl, zh] + zin[0, 7].astype(F32) + zin[1, 7].astype(F32)
    out[...] = mixed[:, 0:EIGHTH].astype(BF16)

    block_a, block_b = buf_a.at[0, 0], buf_b.at[0, 0]
    sent(block_a, ax_s.at[0])
    sent(block_a, ax_s.at[1])
    sent(block_a.at[low], ax_s.at[2])
    sent(block_a.at[low], ax_s.at[3])
    sent(block_b.at[low], bz_s.at[7])
    sent(block_b.at[low], bz_s.at[8])
    sent(w_gate.at[0], w_s.at[0])
    sent(w_up.at[0], w_s.at[1])
    sent(cnt, c_s)
    sent(wd_lanes(0, 0), wf_s.at[0])
    for k in (1, 2, 3):
        sent(w_down.at[0], wd_s.at[k])
        sent(wd_lanes(0, 0), wf_s.at[k])
    for side in range(2):
        sent(zout.at[side, 0, low], z_s.at[side, 0])

    def drain(j, carry):
        sent(block_b, bx_s.at[j, 0])
        sent(block_b, bx_s.at[j, 1])
        sent(block_b.at[low], bx_s.at[j, 2])
        sent(block_b.at[low], bx_s.at[j, 3])
        for k in (1, 2, 3):
            sent(hid.at[0, 0], h_s.at[j, k])
        for i in range(2):
            sent(xin1.at[0, 0], x1_s.at[j, i])
            sent(xin2.at[0, 0], x2_s.at[j, i])

        @pl.when(j >= 1)
        def _():
            for q in range(4):
                sent(block_a, az_s.at[j, q])
            for side in range(2):
                sent(zout.at[0, 0], z_s.at[side, j])

        @pl.when((j >= 1) & (j <= 6))
        def _():
            sent(block_b, bz_s.at[j])

        return carry

    lax.fori_loop(0, SLABS, drain, 0)


def per_device(tokens, expert_ids, router_gates, replica_plan, w_gate, w_up, w_down):
    anywhere = pl.BlockSpec(memory_space=pl.ANY)
    vmem = pl.BlockSpec(memory_space=pltpu.VMEM)
    sem = pltpu.SemaphoreType.DMA
    mixed, load = pl.pallas_call(
        kernel,
        out_shape=(
            jax.ShapeDtypeStruct((ROWS, EIGHTH), BF16),
            jax.ShapeDtypeStruct((8, 128), F32),
        ),
        in_specs=[
            anywhere, vmem, vmem, pl.BlockSpec(memory_space=pltpu.SMEM),
            anywhere, anywhere, anywhere,
        ],
        out_specs=(vmem, vmem),
        scratch_shapes=[
            pltpu.VMEM((8, 4, ROWS, WA), BF16),
            pltpu.VMEM((8, 4, ROWS, WB + EXTRA), BF16),
            pltpu.VMEM((D, 512), BF16),
            pltpu.VMEM((2, PADDED, 1024), BF16),
            pltpu.VMEM((8, 4, 128, 256), BF16),
            pltpu.VMEM((8, 2, 4, ROWS, PADDED), BF16),
            pltpu.VMEM((8, 2, 2, HALF, PADDED), BF16),
            pltpu.VMEM((8, 2, 2, ROWS, PADDED), BF16),
            pltpu.VMEM((8, 2, ROWS, PADDED), F32),
            pltpu.VMEM((2, 8, ROWS, PADDED), BF16),
            pltpu.VMEM((2, 8, ROWS, PADDED), BF16),
            pltpu.VMEM((8, 128), F32),
            pltpu.VMEM((8, 128), F32),
            sem((5,)),
            sem((2,)), sem((2,)),
            sem((4,)), sem((4,)),
            sem((4,)), sem((4,)),
            sem((4,)), sem((4,)),
            sem((8, 4)), sem((8, 4)),
            sem((9,)), sem((9,)),
            sem((8, 4)), sem((8, 4)),
            sem((8, 4)), sem((8, 4)),
            sem((8, 2)), sem((8, 2)),
            sem((8, 2)), sem((8, 2)),
            sem((2, 8)), sem((2, 8)),
            sem, sem,
        ],
        compiler_params=pltpu.CompilerParams(
            collective_id=0, has_side_effects=True, vmem_limit_bytes=48 * 1024 * 1024
        ),
        cost_estimate=pl.CostEstimate(
            flops=6_000_000_000, bytes_accessed=4_000_000, transcendentals=300_000
        ),
    )(
        tokens,
        expert_ids,
        router_gates,
        replica_plan,
        w_gate,
        w_up,
        w_down.reshape(4, 2, EIGHTH, 128),
    )
    return mixed, load[0, 0:1]


def solution(mesh):
    placed = (
        P("expert", None),
        P("expert", None),
        P("expert", None),
        P(),
        P("expert", None, "dp"),
        P("expert", None, "dp"),
        P("expert", None, "dp"),
    )
    return jax.shard_map(
        per_device,
        mesh=mesh,
        in_specs=placed,
        out_specs=(P("expert", "dp"), P("expert")),
        check_vma=False,
    )
```

time: 913 us -> 122 us (0.13)
  the two profiles are of different devices: /device:TPU:8 before, /device:TPU:6 now
where the time goes in v2:
time: 122 us
  Pallas kernels  114 us (93%)
  local copies, waits for them, and re-layouts  7.03 us (6%)
    pallas_call x1, Pallas kernels, per_device(): pl.pallas_call(kernel, out_shape=(jax.ShapeDtypeStruct((ROWS, EIGHTH), BF...  114 us
    unnamed x15, local copies, waits for them, and re-layouts  6.51 us

profile of v2, /device:TPU:6, one launch (start us, length us, event | category | flops | bytes accessed | tf_op | source)
XLA Modules:
  0.0 122.1 jit_solution(1446253194735840983)
XLA Ops:
  0.6 0.0 copy-start.5
  0.6 0.8 copy.9.ids
  1.4 0.0 copy-done.5
  1.4 0.0 copy-start.4
  1.4 0.1 copy.10.gates
  1.5 0.6 copy-done.4
  2.1 0.0 copy-start
  2.1 1.2 copy-done
  3.2 0.0 copy-start.1
  3.2 1.2 copy-done.1
  4.4 0.0 copy-start.2
  4.4 1.2 copy-done.2
  5.6 0.0 copy-start.3
  5.6 0.9 copy-done.3
  6.5 114.4 %shard_map.86 = (bf16[32,448]{1,0:T(8,128)(2,1)S(1)}, f32[8,128]{1,0:T(8,128)S(1)}) custom-call(bf16[32,3584]{1,0:T(8,128)(2,1)S(1)} %copy-done.3, s32[32,8]{1,0:T(8,128)S(1)} %copy.9.ids, f32[32,8]{1,0:T(8,128)S(1)} %copy.10.gates, s32[64]{0:T(128)S(1)} %copy-done.4, bf16[1,3584,128]{2,1,0:T(8,128)(2,1)S(1)} %copy-done, ...), custom_call_target="tpu_custom_call" | custom-call | flops 6000000000 | bytes 4000000 | tf_op jit(solution)/shard_map/pallas_call | solution.py:444
  121.0 0.5 slice.3
  121.5 0.6 copy.12
Async XLA Ops:
  0.6 0.8 copy-start.5
  1.4 0.7 copy-start.4
  2.1 1.2 copy-start
  3.2 1.2 copy-start.1
  4.4 1.2 copy-start.2
  5.6 0.9 copy-start.3

commit v3 on v2

v3 whole, which is shorter than its diff:
```python
import jax
import jax.numpy as jnp
from jax import lax
from jax.experimental import pallas as pl
from jax.experimental.pallas import tpu as pltpu
from jax.sharding import PartitionSpec as P

BF16, F32 = jnp.bfloat16, jnp.float32
ROWS, HALF = 32, 16
D = 3584
WA = 1792
WB = D - WA
EXTRA = 128
CAP = 4
SLABS = 8
QUARTER, EIGHTH, PADDED = 896, 448, 512


def kernel(
    tokens, ids, gates, plan, w_gate, w_up, w_down,
    out, load,
    buf_a, buf_b, wgu, wd, hid, part, xin1, xin2, xin3, xr, zin, zout, cnt, cnt_in,
    loc, w_s, w_r, wd_s, wd_r, wf_s, wf_r, ax_s, ax_r, az_s, az_r, bz_s, bz_r, bx_s, bx_r,
    h_s, h_r, x1_s, x1_r, x2_s, x2_r, z_s, z_r, c_s, c_r,
):
    dp = lax.axis_index("dp")
    ex = lax.axis_index("expert")
    y, zh = lax.div(dp, 2), lax.rem(dp, 2)
    x, zl, core = lax.div(ex, 16), lax.rem(lax.div(ex, 2), 8), lax.rem(ex, 2)
    z = zh * 8 + zl

    def at_x(dx):
        return (dp, ex + (lax.rem(x + dx + 4, 4) - x) * 16)

    def at_y(dy):
        return (lax.rem(y + dy, 4) * 2 + zh, ex)

    def at_z(dz):
        new = lax.rem(z + dz + 16, 16)
        return (y * 2 + lax.div(new, 8), ex + (lax.rem(new, 8) - zl) * 2)

    peer = (dp, ex + 1 - 2 * core)

    def send(src, dst, ss, rs, dev):
        pltpu.make_async_remote_copy(
            src_ref=src, dst_ref=dst, send_sem=ss, recv_sem=rs, device_id=dev,
            device_id_type=pl.DeviceIdType.MESH,
        ).start()

    def arrived(ref, sem):
        pltpu.make_async_remote_copy(
            src_ref=ref, dst_ref=ref, send_sem=sem, recv_sem=sem, device_id=peer,
            device_id_type=pl.DeviceIdType.MESH,
        ).wait_recv()

    def sent(ref, sem):
        pltpu.make_async_remote_copy(
            src_ref=ref, dst_ref=ref, send_sem=sem, recv_sem=sem, device_id=peer,
            device_id_type=pl.DeviceIdType.MESH,
        ).wait_send()

    def xs(q):
        return lax.rem(x + (0, 3, 1, 2)[q], 4)

    def label(j):
        return lax.rem(zl + (1 - 2 * lax.rem(j, 2)) * lax.div(j + 1, 2) + 8, 8)

    low, high = pl.ds(0, HALF), pl.ds(HALF, HALF)
    core_lanes = pl.multiple_of(core * 256, 128)

    own_a, own_b = buf_a.at[zl, x], buf_b.at[zl, x]
    local = [
        pltpu.make_async_copy(tokens.at[:, pl.ds(0, WA)], own_a, loc.at[0]),
        pltpu.make_async_copy(tokens.at[:, pl.ds(WA, WB)], own_b.at[:, pl.ds(0, WB)], loc.at[1]),
        pltpu.make_async_copy(w_gate.at[0], wgu.at[:, pl.ds(core_lanes, 128)], loc.at[2]),
        pltpu.make_async_copy(w_up.at[0], wgu.at[:, pl.ds(core_lanes + 128, 128)], loc.at[3]),
        pltpu.make_async_copy(
            w_down.at[y],
            wd.at[:, pl.ds(0, EIGHTH), pl.ds(pl.multiple_of((y * 2 + core) * 128, 128), 128)],
            loc.at[4],
        ),
    ]
    for copy in local:
        copy.start()

    barrier = pltpu.get_barrier_semaphore()
    partners = [at_x(1), at_x(-1), at_x(2)]
    partners += [at_z(step) for step in (1, -1, 2, -2, 3, -3, 4, -4)]
    partners += [at_y(1), at_y(2), at_y(3), peer]
    for dev in partners:
        pl.semaphore_signal(barrier, inc=1, device_id=dev, device_id_type=pl.DeviceIdType.MESH)

    wd[:, pl.ds(EIGHTH, PADDED - EIGHTH), :] = jnp.zeros((2, PADDED - EIGHTH, 1024), BF16)
    cnt[...] = jnp.zeros_like(cnt)
    local[0].wait()
    pl.semaphore_wait(barrier, len(partners))

    def send_az(jd, q):
        odd = lax.rem(jd, 2) == 1
        up = odd if q < 2 else (odd & (jd != 7))
        way = jnp.where(up, 1, -1)
        ref = buf_a.at[lax.rem(zl - way * (lax.div(jd + 1, 2) - 1) + 8, 8), xs(q)]
        send(ref, ref, az_s, az_r.at[jd, q], at_z(way))

    def send_bz(jd, up, rows, sem):
        way = 1 if up is True else -1 if up is False else jnp.where(up, 1, -1)
        ref = buf_b.at[lax.rem(zl - way * (lax.div(jd + 1, 2) - 1) + 8, 8), x, rows]
        send(ref, ref, bz_s.at[sem], bz_r.at[sem], at_z(way))

    def send_bx(j):
        ref = buf_b.at[label(j), x]
        send(ref, ref, bx_s, bx_r.at[j, 0], at_x(1))
        send(ref, ref, bx_s, bx_r.at[j, 1], at_x(-1))

    whole = pl.ds(0, ROWS)
    send(own_a, own_a, ax_s.at[0], ax_r.at[0], at_x(1))
    send(own_a, own_a, ax_s.at[1], ax_r.at[1], at_x(-1))
    send_az(jnp.int32(1), 0)
    send_az(jnp.int32(2), 0)
    for i, src in enumerate((w_gate, w_up)):
        dst = wgu.at[:, pl.ds(core_lanes + 128 * i, 128)]
        send(src.at[0], dst, w_s.at[i], w_r.at[i], peer)

    def wd_lanes(row_block, which):
        return wd.at[
            :, pl.ds(0, EIGHTH), pl.ds(pl.multiple_of((row_block * 2 + which) * 128, 128), 128)
        ]

    for k in (1, 2, 3):
        send(
            w_down.at[lax.rem(y + k, 4)], wd_lanes(y, core), wd_s.at[k], wd_r.at[k], at_y(k)
        )

    part_row = lax.broadcasted_iota(jnp.int32, (EXTRA, ROWS), 0)
    expert_row = jnp.where(part_row >= 64, part_row - 64, part_row)
    chosen = jnp.zeros((EXTRA, ROWS), F32)
    weight = jnp.zeros((EXTRA, ROWS), F32)
    for k in range(8):
        hit = ids[k : k + 1, :] == expert_row
        chosen = chosen + jnp.where(hit, 1.0, 0.0)
        weight = weight + jnp.where(hit, gates[k : k + 1, :], 0.0)
    row = lax.broadcasted_iota(jnp.int32, (ROWS, ROWS), 0)
    col = lax.broadcasted_iota(jnp.int32, (ROWS, ROWS), 1)
    earlier = ((row < col) & (((col - row) & 1) == 0)).astype(BF16)
    before = jnp.dot(chosen.astype(BF16), earlier, preferred_element_type=F32)
    weight = jnp.where(before < CAP - 0.5, weight, 0.0)
    coarse = weight.astype(BF16).astype(F32)
    parts = jnp.where(part_row < 64, coarse, weight - coarse).astype(BF16)
    buf_b[zl, x, :, pl.ds(WB, EXTRA)] = lax.dot_general(
        (row == col).astype(BF16), parts, (((1,), (1,)), ((), ())), preferred_element_type=F32
    ).astype(BF16)
    local[1].wait()
    send_bz(jnp.int32(1), True, whole, 1)
    send_bz(jnp.int32(2), False, whole, 2)
    send_bx(jnp.int32(0))

    def first_x():
        one, two = jnp.int32(1), jnp.int32(2)
        ref = buf_a.at[zl, xs(1)]
        arrived(ref, ax_r.at[0])
        send(ref.at[low], ref.at[low], ax_s.at[2], ax_r.at[2], at_x(1))
        send_az(one, 1)
        send_az(two, 1)
        ref = buf_a.at[zl, xs(2)]
        arrived(ref, ax_r.at[1])
        send(ref.at[high], ref.at[high], ax_s.at[3], ax_r.at[3], at_x(-1))
        send_az(one, 2)
        send_az(two, 2)
        arrived(buf_a.at[zl, xs(3), low], ax_r.at[2])
        arrived(buf_a.at[zl, xs(3), high], ax_r.at[3])
        send_az(one, 3)
        send_az(two, 3)

    def along_z(d, q):
        @pl.when((d <= 3) | (q < 2))
        def _():
            jd = 2 * d - 1
            arrived(buf_a.at[label(jd), xs(q)], az_r.at[jd, q])

            @pl.when((d <= 2) | ((d == 3) & (q < 2)))
            def _():
                send_az(jd + 2, q)

        @pl.when((d <= 3) | (q >= 2))
        def _():
            jd = jnp.minimum(2 * d, 7)
            arrived(buf_a.at[label(jd), xs(q)], az_r.at[jd, q])

            @pl.when((d <= 2) | ((d == 3) & (q >= 2)))
            def _():
                send_az(jnp.minimum(jd + 2, 7), q)

    def ahead_z(dist, up):
        side = 0 if up else 1

        @pl.when(dist <= 3)
        def _():
            jd = 2 * dist - 1 + side
            arrived(buf_b.at[label(jd), x], bz_r.at[jd])

            @pl.when(dist <= 2)
            def _():
                send_bz(jd + 2, up, whole, jd + 2)

            @pl.when(dist == 3)
            def _():
                send_bz(jnp.int32(7), up, low if up else high, 7 + side)

            send_bx(jd)

        @pl.when(dist == 4)
        def _():
            jd = jnp.int32(7)
            arrived(buf_b.at[label(jd), x, low if up else high], bz_r.at[7 + side])
            if not up:
                send_bx(jd)

    def along_x(j):
        ref = buf_b.at[label(j), xs(1)]
        arrived(ref, bx_r.at[j, 0])
        send(ref.at[low], ref.at[low], bx_s, bx_r.at[j, 2], at_x(1))
        ref = buf_b.at[label(j), xs(2)]
        arrived(ref, bx_r.at[j, 1])
        send(ref.at[high], ref.at[high], bx_s, bx_r.at[j, 3], at_x(-1))

    def along_x_far(j):
        arrived(buf_b.at[label(j), xs(3), low], bx_r.at[j, 2])
        arrived(buf_b.at[label(j), xs(3), high], bx_r.at[j, 3])

    def experts(j):
        @pl.when(j == 0)
        def _():
            local[2].wait()
            local[3].wait()
            other = pl.multiple_of((1 - core) * 256, 128)
            for i in range(2):
                arrived(wgu.at[:, pl.ds(other + 128 * i, 128)], w_r.at[i])

        slab = label(j)
        acc = jnp.dot(
            buf_a[slab].reshape(128, WA), wgu[pl.ds(0, WA), :], preferred_element_type=F32
        )
        acc = acc + jnp.dot(
            buf_b[slab, :, :, pl.ds(0, WB)].reshape(128, WB),
            wgu[pl.ds(WA, WB), :],
            preferred_element_type=F32,
        )
        mix = buf_b[slab, :, :, pl.ds(WB, EXTRA)].reshape(128, EXTRA)
        lane = lax.broadcasted_iota(jnp.int32, (EXTRA, 256), 0)
        unit = lax.broadcasted_iota(jnp.int32, (EXTRA, 256), 1)
        wanted = (ex - core) + (unit >= 128).astype(jnp.int32)
        pick = ((lane == wanted) | (lane == wanted + 64)).astype(BF16)
        scale = jnp.dot(mix, pick, preferred_element_type=F32)
        gate_out = jnp.concatenate([acc[:, 0:128], acc[:, 256:384]], axis=1)
        up_out = jnp.concatenate([acc[:, 128:256], acc[:, 384:512]], axis=1)
        hidden = gate_out / (1.0 + jnp.exp(-gate_out)) * up_out * scale
        hid[slab, y] = hidden.astype(BF16)
        for k in (1, 2, 3):
            ref = hid.at[slab, y]
            send(ref, ref, h_s, h_r.at[j, k], at_y(k))
        kept = jnp.where(mix.astype(F32) > 0.0, 1.0, 0.0).astype(BF16)
        r = lax.broadcasted_iota(jnp.int32, (8, 128), 0)
        t = lax.broadcasted_iota(jnp.int32, (8, 128), 1)
        parity = (r == (t & 1)).astype(BF16)
        cnt[...] += jnp.dot(parity, kept, preferred_element_type=F32)

    def pass_down_weights():
        local[4].wait()
        ref = wd_lanes(y, core)
        send(ref, ref, wf_s.at[0], wf_r.at[0], peer)
        for k in (1, 2, 3):
            ref = wd_lanes(lax.rem(y - k + 4, 4), core)
            arrived(ref, wd_r.at[k])
            send(ref, ref, wf_s.at[k], wf_r.at[k], peer)

    def down(j):
        @pl.when(j == 0)
        def _():
            for k in range(4):
                arrived(wd_lanes(lax.rem(y - k + 4, 4), 1 - core), wf_r.at[k])

        slab = label(j)
        for k in (1, 2, 3):
            arrived(hid.at[slab, lax.rem(y - k + 4, 4)], h_r.at[j, k])
        joined = jnp.concatenate([hid[slab, i] for i in range(4)], axis=1)
        for side in range(2):
            value = lax.dot_general(
                joined, wd[side], (((1,), (1,)), ((), ())), preferred_element_type=F32
            )
            part[slab, side] = value.astype(BF16).reshape(4, ROWS, PADDED)
        far = part.at[slab, :, xs(3)]

        @pl.when(j < 7)
        def _():
            send(far.at[:, low], xin1.at[j, 0], x1_s, x1_r.at[j, 0], at_x(1))
            send(far.at[:, high], xin1.at[j, 1], x1_s, x1_r.at[j, 1], at_x(-1))

        @pl.when(j == 7)
        def _():
            send(far, xin3, x1_s, x1_r.at[j, 0], at_x(2))
            send(part.at[slab, :, xs(2)], xin2.at[j, 0], x2_s, x2_r.at[j, 0], at_x(1))
            send(part.at[slab, :, xs(1)], xin2.at[j, 1], x2_s, x2_r.at[j, 1], at_x(-1))

    def add_far(j):
        slab = label(j)
        for i, (q, rows, step) in enumerate(((2, low, 1), (1, high, -1))):
            arrived(xin1.at[j, i], x1_r.at[j, i])
            there = part[slab, :, xs(q), rows, :].astype(F32) + xin1[j, i].astype(F32)
            part[slab, :, xs(q), rows, :] = there.astype(BF16)
            send(part.at[slab, :, xs(q)], xin2.at[j, i], x2_s, x2_r.at[j, i], at_x(step))

    def z_step(s, way, side, kind):
        slab = lax.rem(zl - s * way + 8, 8)
        half = lax.div(lax.rem(z + way * (8 - s) + 16, 16), 8)
        value = xr[slab, half]
        rows = low if side == 0 else high
        if kind == "first":
            zout[side, s] = value.astype(BF16)
            send(
                zout.at[side, s, rows], zin.at[side, s, rows],
                z_s.at[side, s], z_r.at[side, s], at_z(way),
            )
            return
        if kind == "second":
            arrived(zin.at[side, s - 1, rows], z_r.at[side, s - 1])
            zout[side, s] = value.astype(BF16)
            more = xr[slab, half, rows, :] + zin[side, s - 1, rows, :].astype(F32)
            zout[side, s, rows, :] = more.astype(BF16)
        elif kind == "alone":
            zout[side, s] = value.astype(BF16)
        else:
            arrived(zin.at[side, s - 1], z_r.at[side, s - 1])
            zout[side, s] = (value + zin[side, s - 1].astype(F32)).astype(BF16)
        there = at_z(way if kind in ("second", "on") else (8 - s) * way)
        send(zout.at[side, s], zin.at[side, s], z_s.at[side, s], z_r.at[side, s], there)

    def both(s, kind):
        z_step(s, 1, 0, kind)
        z_step(s, -1, 1, kind)

    def add_near(j):
        slab = label(j)
        arrived(xin2.at[j, 0], x2_r.at[j, 0])
        arrived(xin2.at[j, 1], x2_r.at[j, 1])
        xr[slab] = (
            part[slab, :, x].astype(F32) + xin2[j, 0].astype(F32) + xin2[j, 1].astype(F32)
        )

        @pl.when(j == 7)
        def _():
            arrived(xin3, x1_r.at[j, 0])
            xr[slab] = xr[slab] + xin3[...].astype(F32)

    def slabs(d, work):
        def one(j, carry):
            work(j)
            return carry

        lax.fori_loop(jnp.maximum(2 * d - 1, 0), jnp.minimum(2 * d, 7) + 1, one, 0)

    def turn(d, carry):
        @pl.when(d == 0)
        def _():
            first_x()
            ahead_z(jnp.int32(1), True)
            ahead_z(jnp.int32(1), False)

        for q in range(4):

            @pl.when(d >= 1)
            def _():
                along_z(d, q)

            if q == 0:
                along_x(jnp.maximum(2 * d - 1, 0))

            if q == 1:

                @pl.when((d >= 1) & (d <= 3))
                def _():
                    along_x(2 * d)

                @pl.when(d >= 2)
                def _():
                    slabs(d - 2, add_far)

            if q >= 2:

                @pl.when(d <= 2)
                def _():
                    ahead_z(d + 2, q == 2)

            if q == 2:

                @pl.when(d == 1)
                def _():
                    pass_down_weights()

                @pl.when(d == 4)
                def _():
                    slabs(d - 1, down)

            if q == 3:

                @pl.when(d >= 2)
                def _():
                    slabs(d - 2, add_near)

                    @pl.when(d == 2)
                    def _():
                        both(0, "first")

                    @pl.when(d == 3)
                    def _():
                        both(1, "second")
                        both(7, "alone")

                    @pl.when(d == 4)
                    def _():
                        both(2, "on")
                        both(6, "alone")
                        slabs(d - 1, add_far)

                slabs(d, along_x_far)

        slabs(d, experts)

        @pl.when((d >= 1) & (d <= 3))
        def _():
            slabs(d - 1, down)

        return carry

    lax.fori_loop(0, 5, turn, 0)
    send(cnt, cnt_in, c_s, c_r, peer)
    slabs(jnp.int32(3), add_near)
    both(3, "on")
    both(5, "alone")
    down(jnp.int32(7))
    add_near(jnp.int32(7))
    both(4, "straight")

    arrived(cnt_in, c_r)
    total = cnt[...] + cnt_in[...]
    r = lax.broadcasted_iota(jnp.int32, (8, 128), 0)
    t = lax.broadcasted_iota(jnp.int32, (8, 128), 1)
    copied = plan[ex]
    served = ((r == 0) & (t == ex)) | ((r == 1) & (t == copied))
    load[0] = jnp.sum(jnp.where(served, total, 0.0)) * (1.0 / 256.0)

    mixed = xr[zl, zh]
    for step in (7, 6, 5, 4):
        for side in range(2):
            arrived(zin.at[side, step], z_r.at[side, step])
            mixed = mixed + zin[side, step].astype(F32)
    out[...] = mixed[:, 0:EIGHTH].astype(BF16)

    block_a, block_b = buf_a.at[0, 0], buf_b.at[0, 0]
    sent(block_a, ax_s.at[0])
    sent(block_a, ax_s.at[1])
    sent(block_a.at[low], ax_s.at[2])
    sent(block_a.at[low], ax_s.at[3])
    sent(block_b.at[low], bz_s.at[7])
    sent(block_b.at[low], bz_s.at[8])
    for jd in range(1, 7):
        sent(block_b, bz_s.at[jd])
    sent(buf_a.at[pl.ds(0, 7)], az_s)
    sent(buf_b.at[pl.ds(0, 6)], bx_s)
    sent(hid.at[pl.ds(0, 6)], h_s)
    sent(hid.at[pl.ds(0, 2)], x1_s)
    sent(hid.at[pl.ds(0, 4)], x2_s)
    sent(w_gate.at[0], w_s.at[0])
    sent(w_up.at[0], w_s.at[1])
    sent(cnt, c_s)
    sent(wd_lanes(0, 0), wf_s.at[0])
    for k in (1, 2, 3):
        sent(w_down.at[0], wd_s.at[k])
        sent(wd_lanes(0, 0), wf_s.at[k])
    for side in range(2):
        sent(zout.at[side, 0, low], z_s.at[side, 0])
        for step in range(1, 8):
            sent(zout.at[side, step], z_s.at[side, step])


def per_device(tokens, expert_ids, router_gates, replica_plan, w_gate, w_up, w_down):
    hbm = pl.BlockSpec(memory_space=pltpu.HBM)
    smem = pl.BlockSpec(memory_space=pltpu.SMEM)
    vmem = pl.BlockSpec(memory_space=pltpu.VMEM)
    sem = pltpu.SemaphoreType.DMA
    mixed, load = pl.pallas_call(
        kernel,
        out_shape=(
            jax.ShapeDtypeStruct((ROWS, EIGHTH), BF16),
            jax.ShapeDtypeStruct((1,), F32),
        ),
        in_specs=[
            hbm, vmem, vmem, smem, hbm, hbm, hbm,
        ],
        out_specs=(vmem, smem),
        scratch_shapes=[
            pltpu.VMEM((8, 4, ROWS, WA), BF16),
            pltpu.VMEM((8, 4, ROWS, WB + EXTRA), BF16),
            pltpu.VMEM((D, 512), BF16),
            pltpu.VMEM((2, PADDED, 1024), BF16),
            pltpu.VMEM((8, 4, 128, 256), BF16),
            pltpu.VMEM((8, 2, 4, ROWS, PADDED), BF16),
            pltpu.VMEM((8, 2, 2, HALF, PADDED), BF16),
            pltpu.VMEM((8, 2, 2, ROWS, PADDED), BF16),
            pltpu.VMEM((2, ROWS, PADDED), BF16),
            pltpu.VMEM((8, 2, ROWS, PADDED), F32),
            pltpu.VMEM((2, 8, ROWS, PADDED), BF16),
            pltpu.VMEM((2, 8, ROWS, PADDED), BF16),
            pltpu.VMEM((8, 128), F32),
            pltpu.VMEM((8, 128), F32),
            sem((5,)),
            sem((2,)), sem((2,)),
            sem((4,)), sem((4,)),
            sem((4,)), sem((4,)),
            sem((4,)), sem((4,)),
            sem, sem((8, 4)),
            sem((9,)), sem((9,)),
            sem, sem((8, 4)),
            sem, sem((8, 4)),
            sem, sem((8, 2)),
            sem, sem((8, 2)),
            sem((2, 8)), sem((2, 8)),
            sem, sem,
        ],
        compiler_params=pltpu.CompilerParams(
            collective_id=0, has_side_effects=True, vmem_limit_bytes=60 * 1024 * 1024
        ),
        cost_estimate=pl.CostEstimate(
            flops=6_000_000_000, bytes_accessed=4_000_000, transcendentals=300_000
        ),
    )(
        tokens,
        expert_ids.T,
        router_gates.T,
        replica_plan,
        w_gate,
        w_up,
        w_down.reshape(4, 2, EIGHTH, 128),
    )
    return mixed, load


def solution(mesh):
    placed = (
        P("expert", None),
        P("expert", None),
        P("expert", None),
        P(),
        P("expert", None, "dp"),
        P("expert", None, "dp"),
        P("expert", None, "dp"),
    )
    return jax.shard_map(
        per_device,
        mesh=mesh,
        in_specs=placed,
        out_specs=(P("expert", "dp"), P("expert")),
        check_vma=False,
    )
```

time: 122 us -> 97.4 us (0.80)
  Pallas kernels: 114 us -> 92.7 us
  local copies, waits for them, and re-layouts: 7.03 us -> 1.38 us
  between operations: 0.65 us -> 2.4 us
    pallas_call x1, Pallas kernels: 114 us -> 92.7 us  [per_device(): pl.pallas_call(kernel, out_shape=(jax.ShapeDtypeStruct((ROWS, EIGHTH), BF...]
    unnamed x15 -> x1, local copies, waits for them, and re-layouts: 6.51 us -> 1.38 us
where the time goes in v3:
time: 97.4 us; the launch traced here: 96.5 us
  Pallas kernels  92.7 us (95%)
  between operations  2.4 us (2%)
  local copies, waits for them, and re-layouts  1.38 us (1%)
    pallas_call x1, Pallas kernels, per_device(): pl.pallas_call(kernel, out_shape=(jax.ShapeDtypeStruct((ROWS, EIGHTH), BF...  92.7 us

profile of v3, /device:TPU:6, one launch (start us, length us, event | category | flops | bytes accessed | tf_op | source)
XLA Modules:
  0.0 96.5 jit_solution(11723945215062646302)
XLA Ops:
  0.6 92.7 %shard_map.86 = (bf16[32,448]{1,0:T(8,128)(2,1)}, f32[1]{0:T(128)}) custom-call(bf16[32,3584]{1,0:T(8,128)(2,1)} %tokens.1, s32[8,32]{1,0:T(8,128)} %bitcast.4, f32[8,32]{1,0:T(8,128)} %bitcast.5, s32[64]{0:T(128)} %plan.1, bf16[1,3584,128]{2,1,0:T(8,128)(2,1)} %w_gate.1, bf16[1,3584,128]{2,1,0:T(8,128)(2,1)} %w_up.1, bf16[4,2,448,128]{3,2,1,0:T(8,128)(2,1)} %bitcast.3), custom_call_target="tpu_custom_call" | custom-call | flops 6000000000 | bytes 4000000 | tf_op jit(solution)/shard_map/pallas_call | solution.py:490
  93.3 1.4 %copy.11 = bf16[32,448]{1,0:T(8,128)(2,1)} copy(bf16[32,448]{1,0:T(8,128)(2,1)} %get-tuple-element.4) | data formatting | bytes 57344

commit v4 on v3

--- a/solution.py
+++ b/solution.py
@@ -8,9 +8,11 @@
 BF16, F32 = jnp.bfloat16, jnp.float32
 ROWS, HALF = 32, 16
 D = 3584
-WA = 1792
-WB = D - WA
+WC = 256
+WA = 1536
+WB = D - WA - 4 * WC
 EXTRA = 128
+SLOTS = 32
 CAP = 4
 SLABS = 8
 QUARTER, EIGHTH, PADDED = 896, 448, 512
@@ -19,9 +21,9 @@
 def kernel(
     tokens, ids, gates, plan, w_gate, w_up, w_down,
     out, load,
-    buf_a, buf_b, wgu, wd, hid, part, xin1, xin2, xin3, xr, zin, zout, cnt, cnt_in,
+    buf_a, buf_b, buf_c, wgu, wd, hid, pt, part, xin1, xin2, xin3, xr, zin, zout, cnt, cnt_in,
     loc, w_s, w_r, wd_s, wd_r, wf_s, wf_r, ax_s, ax_r, az_s, az_r, bz_s, bz_r, bx_s, bx_r,
-    h_s, h_r, x1_s, x1_r, x2_s, x2_r, z_s, z_r, c_s, c_r,
+    cc_s, cc_r, h_s, h_r, x1_s, x1_r, x2_s, x2_r, z_s, z_r, c_s, c_r,
 ):
     dp = lax.axis_index("dp")
     ex = lax.axis_index("expert")
@@ -29,15 +31,23 @@
     x, zl, core = lax.div(ex, 16), lax.rem(lax.div(ex, 2), 8), lax.rem(ex, 2)
     z = zh * 8 + zl
 
+    known = {}
+
     def at_x(dx):
-        return (dp, ex + (lax.rem(x + dx + 4, 4) - x) * 16)
+        if ("x", dx) not in known:
+            known["x", dx] = (dp, ex + (lax.rem(x + dx + 4, 4) - x) * 16)
+        return known["x", dx]
 
     def at_y(dy):
-        return (lax.rem(y + dy, 4) * 2 + zh, ex)
+        if ("y", dy) not in known:
+            known["y", dy] = (lax.rem(y + dy, 4) * 2 + zh, ex)
+        return known["y", dy]
 
     def at_z(dz):
-        new = lax.rem(z + dz + 16, 16)
-        return (y * 2 + lax.div(new, 8), ex + (lax.rem(new, 8) - zl) * 2)
+        if ("z", dz) not in known:
+            new = lax.rem(z + dz + 16, 16)
+            known["z", dz] = (y * 2 + lax.div(new, 8), ex + (lax.rem(new, 8) - zl) * 2)
+        return known["z", dz]
 
     peer = (dp, ex + 1 - 2 * core)
 
@@ -59,11 +69,21 @@
             device_id_type=pl.DeviceIdType.MESH,
         ).wait_send()
 
+    blocks = [lax.rem(x + step, 4) for step in (0, 3, 1, 2)]
+    quarters = [lax.rem(y - k + 4, 4) for k in range(4)]
+
     def xs(q):
-        return lax.rem(x + (0, 3, 1, 2)[q], 4)
-
-    def label(j):
-        return lax.rem(zl + (1 - 2 * lax.rem(j, 2)) * lax.div(j + 1, 2) + 8, 8)
+        return blocks[q]
+
+    def wrap(place):
+        place = jnp.where(place < 0, place + 8, place)
+        return jnp.where(place >= 8, place - 8, place)
+
+    def label(d, side):
+        return wrap(zl + (2 * side - 1) * d)
+
+    def turn_of(d, side):
+        return 2 * d - 1 + side
 
     low, high = pl.ds(0, HALF), pl.ds(HALF, HALF)
     core_lanes = pl.multiple_of(core * 256, 128)
@@ -76,8 +96,13 @@
         pltpu.make_async_copy(w_up.at[0], wgu.at[:, pl.ds(core_lanes + 128, 128)], loc.at[3]),
         pltpu.make_async_copy(
             w_down.at[y],
-            wd.at[:, pl.ds(0, EIGHTH), pl.ds(pl.multiple_of((y * 2 + core) * 128, 128), 128)],
+            wd.at[:, pl.ds(0, EIGHTH), pl.ds(pl.multiple_of((core * 4 + y) * 128, 128), 128)],
             loc.at[4],
+        ),
+        pltpu.make_async_copy(
+            tokens.at[:, pl.ds(pl.multiple_of(WA + WB + y * WC, 128), WC)],
+            own_b.at[:, pl.ds(WB + EXTRA, WC)],
+            loc.at[5],
         ),
     ]
     for copy in local:
@@ -95,35 +120,34 @@
     local[0].wait()
     pl.semaphore_wait(barrier, len(partners))
 
-    def send_az(jd, q):
-        odd = lax.rem(jd, 2) == 1
-        up = odd if q < 2 else (odd & (jd != 7))
-        way = jnp.where(up, 1, -1)
-        ref = buf_a.at[lax.rem(zl - way * (lax.div(jd + 1, 2) - 1) + 8, 8), xs(q)]
+    def send_az(dist, side, q):
+        way = 1 - 2 * side
+        ref = buf_a.at[wrap(zl - way * (dist - 1)), xs(q)]
+        jd = jnp.minimum(turn_of(dist, side), 7)
         send(ref, ref, az_s, az_r.at[jd, q], at_z(way))
 
-    def send_bz(jd, up, rows, sem):
-        way = 1 if up is True else -1 if up is False else jnp.where(up, 1, -1)
-        ref = buf_b.at[lax.rem(zl - way * (lax.div(jd + 1, 2) - 1) + 8, 8), x, rows]
+    def send_bz(dist, side, rows, sem):
+        way = 1 - 2 * side
+        ref = buf_b.at[wrap(zl - way * (dist - 1)), x, rows]
         send(ref, ref, bz_s.at[sem], bz_r.at[sem], at_z(way))
 
-    def send_bx(j):
-        ref = buf_b.at[label(j), x]
+    def send_bx(d, side):
+        ref, j = buf_b.at[label(d, side), x], turn_of(d, side)
         send(ref, ref, bx_s, bx_r.at[j, 0], at_x(1))
         send(ref, ref, bx_s, bx_r.at[j, 1], at_x(-1))
 
     whole = pl.ds(0, ROWS)
     send(own_a, own_a, ax_s.at[0], ax_r.at[0], at_x(1))
     send(own_a, own_a, ax_s.at[1], ax_r.at[1], at_x(-1))
-    send_az(jnp.int32(1), 0)
-    send_az(jnp.int32(2), 0)
+    send_az(1, 0, 0)
+    send_az(1, 1, 0)
     for i, src in enumerate((w_gate, w_up)):
         dst = wgu.at[:, pl.ds(core_lanes + 128 * i, 128)]
         send(src.at[0], dst, w_s.at[i], w_r.at[i], peer)
 
     def wd_lanes(row_block, which):
         return wd.at[
-            :, pl.ds(0, EIGHTH), pl.ds(pl.multiple_of((row_block * 2 + which) * 128, 128), 128)
+            :, pl.ds(0, EIGHTH), pl.ds(pl.multiple_of((which * 4 + row_block) * 128, 128), 128)
         ]
 
     for k in (1, 2, 3):
@@ -150,84 +174,85 @@
         (row == col).astype(BF16), parts, (((1,), (1,)), ((), ())), preferred_element_type=F32
     ).astype(BF16)
     local[1].wait()
-    send_bz(jnp.int32(1), True, whole, 1)
-    send_bz(jnp.int32(2), False, whole, 2)
-    send_bx(jnp.int32(0))
+    local[5].wait()
+    send_bz(1, 0, whole, 1)
+    send_bz(1, 1, whole, 2)
+    send_bx(0, 1)
 
     def first_x():
-        one, two = jnp.int32(1), jnp.int32(2)
         ref = buf_a.at[zl, xs(1)]
         arrived(ref, ax_r.at[0])
         send(ref.at[low], ref.at[low], ax_s.at[2], ax_r.at[2], at_x(1))
-        send_az(one, 1)
-        send_az(two, 1)
+        send_az(1, 0, 1)
+        send_az(1, 1, 1)
         ref = buf_a.at[zl, xs(2)]
         arrived(ref, ax_r.at[1])
         send(ref.at[high], ref.at[high], ax_s.at[3], ax_r.at[3], at_x(-1))
-        send_az(one, 2)
-        send_az(two, 2)
+        send_az(1, 0, 2)
+        send_az(1, 1, 2)
         arrived(buf_a.at[zl, xs(3), low], ax_r.at[2])
         arrived(buf_a.at[zl, xs(3), high], ax_r.at[3])
-        send_az(one, 3)
-        send_az(two, 3)
+        send_az(1, 0, 3)
+        send_az(1, 1, 3)
 
     def along_z(d, q):
-        @pl.when((d <= 3) | (q < 2))
-        def _():
-            jd = 2 * d - 1
-            arrived(buf_a.at[label(jd), xs(q)], az_r.at[jd, q])
-
-            @pl.when((d <= 2) | ((d == 3) & (q < 2)))
+        for side in range(2):
+            mine = q // 2 == side
+
+            @pl.when((d <= 3) | mine)
             def _():
-                send_az(jd + 2, q)
-
-        @pl.when((d <= 3) | (q >= 2))
-        def _():
-            jd = jnp.minimum(2 * d, 7)
-            arrived(buf_a.at[label(jd), xs(q)], az_r.at[jd, q])
-
-            @pl.when((d <= 2) | ((d == 3) & (q >= 2)))
-            def _():
-                send_az(jnp.minimum(jd + 2, 7), q)
-
-    def ahead_z(dist, up):
-        side = 0 if up else 1
+                jd = jnp.minimum(turn_of(d, side), 7)
+                arrived(buf_a.at[label(d, side), xs(q)], az_r.at[jd, q])
+
+                @pl.when((d <= 2) | ((d == 3) & mine))
+                def _():
+                    send_az(d + 1, side, q)
+
+    def ahead_z(dist, side):
+        half = high if side else low
 
         @pl.when(dist <= 3)
         def _():
-            jd = 2 * dist - 1 + side
-            arrived(buf_b.at[label(jd), x], bz_r.at[jd])
+            jd = turn_of(dist, side)
+            arrived(buf_b.at[label(dist, side), x], bz_r.at[jd])
 
             @pl.when(dist <= 2)
             def _():
-                send_bz(jd + 2, up, whole, jd + 2)
+                send_bz(dist + 1, side, whole, jd + 2)
 
             @pl.when(dist == 3)
             def _():
-                send_bz(jnp.int32(7), up, low if up else high, 7 + side)
-
-            send_bx(jd)
+                send_bz(4, side, half, 7 + side)
+
+            send_bx(dist, side)
 
         @pl.when(dist == 4)
         def _():
-            jd = jnp.int32(7)
-            arrived(buf_b.at[label(jd), x, low if up else high], bz_r.at[7 + side])
-            if not up:
-                send_bx(jd)
-
-    def along_x(j):
-        ref = buf_b.at[label(j), xs(1)]
+            arrived(buf_b.at[label(4, side), x, half], bz_r.at[7 + side])
+            if side:
+                send_bx(4, 0)
+
+    def along_x(d, side):
+        slab, j = label(d, side), turn_of(d, side)
+        ref = buf_b.at[slab, xs(1)]
         arrived(ref, bx_r.at[j, 0])
         send(ref.at[low], ref.at[low], bx_s, bx_r.at[j, 2], at_x(1))
-        ref = buf_b.at[label(j), xs(2)]
+        ref = buf_b.at[slab, xs(2)]
         arrived(ref, bx_r.at[j, 1])
         send(ref.at[high], ref.at[high], bx_s, bx_r.at[j, 3], at_x(-1))
 
-    def along_x_far(j):
-        arrived(buf_b.at[label(j), xs(3), low], bx_r.at[j, 2])
-        arrived(buf_b.at[label(j), xs(3), high], bx_r.at[j, 3])
-
-    def experts(j):
+    def along_x_far(d, side):
+        slab, j = label(d, side), turn_of(d, side)
+        arrived(buf_b.at[slab, xs(3), low], bx_r.at[j, 2])
+        arrived(buf_b.at[slab, xs(3), high], bx_r.at[j, 3])
+        for k in (1, 2, 3):
+            send(
+                buf_b.at[slab, :, :, pl.ds(WB + EXTRA, WC)], buf_c.at[slab, y],
+                cc_s.at[k], cc_r.at[j, k], at_y(k),
+            )
+
+    def experts(d, side):
+        slab, j = label(d, side), turn_of(d, side)
         @pl.when(j == 0)
         def _():
             local[2].wait()
@@ -236,7 +261,6 @@
             for i in range(2):
                 arrived(wgu.at[:, pl.ds(other + 128 * i, 128)], w_r.at[i])
 
-        slab = label(j)
         acc = jnp.dot(
             buf_a[slab].reshape(128, WA), wgu[pl.ds(0, WA), :], preferred_element_type=F32
         )
@@ -245,6 +269,21 @@
             wgu[pl.ds(WA, WB), :],
             preferred_element_type=F32,
         )
+
+        def quarter(which):
+            return wgu[pl.ds(pl.multiple_of(WA + WB + which * WC, WC), WC), :]
+
+        acc = acc + jnp.dot(
+            buf_b[slab, :, :, pl.ds(WB + EXTRA, WC)].reshape(128, WC),
+            quarter(y),
+            preferred_element_type=F32,
+        )
+        for k in (1, 2, 3):
+            which = quarters[k]
+            arrived(buf_c.at[slab, which], cc_r.at[j, k])
+            acc = acc + jnp.dot(
+                buf_c[slab, which].reshape(128, WC), quarter(which), preferred_element_type=F32
+            )
         mix = buf_b[slab, :, :, pl.ds(WB, EXTRA)].reshape(128, EXTRA)
         lane = lax.broadcasted_iota(jnp.int32, (EXTRA, 256), 0)
         unit = lax.broadcasted_iota(jnp.int32, (EXTRA, 256), 1)
@@ -254,7 +293,24 @@
         gate_out = jnp.concatenate([acc[:, 0:128], acc[:, 256:384]], axis=1)
         up_out = jnp.concatenate([acc[:, 128:256], acc[:, 384:512]], axis=1)
         hidden = gate_out / (1.0 + jnp.exp(-gate_out)) * up_out * scale
-        hid[slab, y] = hidden.astype(BF16)
+        hidden = hidden.astype(BF16)
+        row = lax.broadcasted_iota(jnp.int32, (128, 128), 0)
+        col = lax.broadcasted_iota(jnp.int32, (128, 128), 1)
+        earlier = (col < row) & ((row >> 5) == (col >> 5)) & (((row - col) & 1) == 0)
+        token = lax.broadcasted_iota(jnp.int32, (128, 256), 0)
+        slot = lax.broadcasted_iota(jnp.int32, (128, 256), 1) & 127
+        first = ((token >> 5) * 8 + (token & 1) * 4).astype(F32)
+        served = jnp.where(scale > 0.0, 1.0, 0.0)
+        before = jnp.dot(earlier.astype(BF16), served.astype(BF16), preferred_element_type=F32)
+        place = jnp.where(before + first == slot.astype(F32), served, 0.0).astype(BF16)
+        pt[slab] = place
+        for e in range(2):
+            lanes = slice(e * 128, e * 128 + 128)
+            packed = lax.dot_general(
+                place[:, lanes], hidden[:, lanes], (((0,), (0,)), ((), ())),
+                preferred_element_type=F32,
+            )
+            hid[slab, y, pl.ds(e * SLOTS, SLOTS), :] = packed[0:SLOTS].astype(BF16)
         for k in (1, 2, 3):
             ref = hid.at[slab, y]
             send(ref, ref, h_s, h_r.at[j, k], at_y(k))
@@ -269,20 +325,26 @@
         ref = wd_lanes(y, core)
         send(ref, ref, wf_s.at[0], wf_r.at[0], peer)
         for k in (1, 2, 3):
-            ref = wd_lanes(lax.rem(y - k + 4, 4), core)
+            ref = wd_lanes(quarters[k], core)
             arrived(ref, wd_r.at[k])
             send(ref, ref, wf_s.at[k], wf_r.at[k], peer)
 
-    def down(j):
+    def down(d, side):
+        slab, j = label(d, side), turn_of(d, side)
         @pl.when(j == 0)
         def _():
             for k in range(4):
-                arrived(wd_lanes(lax.rem(y - k + 4, 4), 1 - core), wf_r.at[k])
-
-        slab = label(j)
+                arrived(wd_lanes(quarters[k], 1 - core), wf_r.at[k])
+
         for k in (1, 2, 3):
-            arrived(hid.at[slab, lax.rem(y - k + 4, 4)], h_r.at[j, k])
-        joined = jnp.concatenate([hid[slab, i] for i in range(4)], axis=1)
+            arrived(hid.at[slab, quarters[k]], h_r.at[j, k])
+        spread = []
+        for e in range(2):
+            rows = pl.ds(e * SLOTS, SLOTS)
+            packed = jnp.concatenate([hid[slab, i, rows, :] for i in range(4)], axis=1)
+            place = pt[slab, :, pl.ds(e * 128, 128)][:, 0:SLOTS]
+            spread.append(jnp.dot(place, packed, preferred_element_type=F32).astype(BF16))
+        joined = jnp.concatenate(spread, axis=1)
         for side in range(2):
             value = lax.dot_general(
                 joined, wd[side], (((1,), (1,)), ((), ())), preferred_element_type=F32
@@ -301,17 +363,23 @@
             send(part.at[slab, :, xs(2)], xin2.at[j, 0], x2_s, x2_r.at[j, 0], at_x(1))
             send(part.at[slab, :, xs(1)], xin2.at[j, 1], x2_s, x2_r.at[j, 1], at_x(-1))
 
-    def add_far(j):
-        slab = label(j)
+    def add_far(d, side):
+        slab, j = label(d, side), turn_of(d, side)
         for i, (q, rows, step) in enumerate(((2, low, 1), (1, high, -1))):
             arrived(xin1.at[j, i], x1_r.at[j, i])
             there = part[slab, :, xs(q), rows, :].astype(F32) + xin1[j, i].astype(F32)
             part[slab, :, xs(q), rows, :] = there.astype(BF16)
             send(part.at[slab, :, xs(q)], xin2.at[j, i], x2_s, x2_r.at[j, i], at_x(step))
 
+    halves = {
+        (side, s): lax.div(lax.rem(z + (1 - 2 * side) * (8 - s) + 16, 16), 8)
+        for side in range(2)
+        for s in range(8)
+    }
+
     def z_step(s, way, side, kind):
-        slab = lax.rem(zl - s * way + 8, 8)
-        half = lax.div(lax.rem(z + way * (8 - s) + 16, 16), 8)
+        slab = wrap(zl - s * way)
+        half = halves[side, s]
         value = xr[slab, half]
         rows = low if side == 0 else high
         if kind == "first":
@@ -338,8 +406,8 @@
         z_step(s, 1, 0, kind)
         z_step(s, -1, 1, kind)
 
-    def add_near(j):
-        slab = label(j)
+    def add_near(d, side):
+        slab, j = label(d, side), turn_of(d, side)
         arrived(xin2.at[j, 0], x2_r.at[j, 0])
         arrived(xin2.at[j, 1], x2_r.at[j, 1])
         xr[slab] = (
@@ -351,19 +419,42 @@
             arrived(xin3, x1_r.at[j, 0])
             xr[slab] = xr[slab] + xin3[...].astype(F32)
 
-    def slabs(d, work):
-        def one(j, carry):
-            work(j)
+    def send_c(j):
+        for k in (1, 2, 3):
+            send(
+                buf_b.at[slab, :, :, pl.ds(WB + EXTRA, WC)], buf_c.at[slab, y],
+                cc_s.at[k], cc_r.at[j, k], at_y(k),
+            )
+
+    def pair(d, work):
+        def one(side, carry):
+            work(d, side)
             return carry
 
-        lax.fori_loop(jnp.maximum(2 * d - 1, 0), jnp.minimum(2 * d, 7) + 1, one, 0)
+        lax.fori_loop(0, 2, one, 0)
+
+    def slabs(d, work, least=0, most=4):
+        @pl.when((d >= max(least, 1)) & (d <= most))
+        def _():
+            work(d, 0)
+
+        @pl.when((d >= least) & (d <= min(most, 3)))
+        def _():
+            work(d, 1)
+
+    def loop_slabs(d, work):
+        def one(side, carry):
+            work(d, side)
+            return carry
+
+        lax.fori_loop(jnp.where(d == 0, 1, 0), jnp.where(d == 4, 1, 2), one, 0)
 
     def turn(d, carry):
         @pl.when(d == 0)
         def _():
             first_x()
-            ahead_z(jnp.int32(1), True)
-            ahead_z(jnp.int32(1), False)
+            ahead_z(1, 0)
+            ahead_z(1, 1)
 
         for q in range(4):
 
@@ -372,72 +463,71 @@
                 along_z(d, q)
 
             if q == 0:
-                along_x(jnp.maximum(2 * d - 1, 0))
+
+                @pl.when(d >= 1)
+                def _():
+                    along_x(d, 0)
 
             if q == 1:
 
-                @pl.when((d >= 1) & (d <= 3))
-                def _():
-                    along_x(2 * d)
-
-                @pl.when(d >= 2)
-                def _():
-                    slabs(d - 2, add_far)
+                @pl.when(d <= 3)
+                def _():
+                    along_x(d, 1)
 
             if q >= 2:
 
                 @pl.when(d <= 2)
                 def _():
-                    ahead_z(d + 2, q == 2)
+                    ahead_z(d + 2, q - 2)
 
             if q == 2:
 
+                @pl.when(d >= 1)
+                def _():
+                    loop_slabs(d - 1, experts)
+
                 @pl.when(d == 1)
                 def _():
                     pass_down_weights()
 
-                @pl.when(d == 4)
-                def _():
-                    slabs(d - 1, down)
-
             if q == 3:
-
-                @pl.when(d >= 2)
-                def _():
-                    slabs(d - 2, add_near)
-
-                    @pl.when(d == 2)
+                slabs(d, along_x_far)
+
+                @pl.when(d >= 3)
+                def _():
+                    loop_slabs(d - 3, add_near)
+
+                    @pl.when(d == 3)
                     def _():
                         both(0, "first")
 
-                    @pl.when(d == 3)
+                    @pl.when(d == 4)
                     def _():
                         both(1, "second")
                         both(7, "alone")
 
-                    @pl.when(d == 4)
-                    def _():
-                        both(2, "on")
-                        both(6, "alone")
-                        slabs(d - 1, add_far)
-
-                slabs(d, along_x_far)
-
-        slabs(d, experts)
-
-        @pl.when((d >= 1) & (d <= 3))
-        def _():
-            slabs(d - 1, down)
+                @pl.when(d >= 2)
+                def _():
+                    loop_slabs(d - 2, add_far)
+
+        @pl.when(d >= 1)
+        def _():
+            loop_slabs(d - 1, down)
 
         return carry
 
     lax.fori_loop(0, 5, turn, 0)
+    experts(4, 0)
     send(cnt, cnt_in, c_s, c_r, peer)
-    slabs(jnp.int32(3), add_near)
+    pair(3, add_far)
+    pair(2, add_near)
+    both(2, "on")
+    both(6, "alone")
+    down(4, 0)
+    pair(3, add_near)
     both(3, "on")
     both(5, "alone")
-    down(jnp.int32(7))
-    add_near(jnp.int32(7))
+    add_near(4, 0)
     both(4, "straight")
 
     arrived(cnt_in, c_r)
@@ -466,9 +556,11 @@
         sent(block_b, bz_s.at[jd])
     sent(buf_a.at[pl.ds(0, 7)], az_s)
     sent(buf_b.at[pl.ds(0, 6)], bx_s)
-    sent(hid.at[pl.ds(0, 6)], h_s)
-    sent(hid.at[pl.ds(0, 2)], x1_s)
-    sent(hid.at[pl.ds(0, 4)], x2_s)
+    sent(wd.at[0, pl.ds(0, 192)], h_s)
+    for k in (1, 2, 3):
+        sent(wd.at[0, pl.ds(0, WC)], cc_s.at[k])
+    sent(wd.at[0, pl.ds(0, 256)], x1_s)
+    sent(wd.at[0], x2_s)
     sent(w_gate.at[0], w_s.at[0])
     sent(w_up.at[0], w_s.at[1])
     sent(cnt, c_s)
@@ -499,10 +591,12 @@
         out_specs=(vmem, smem),
         scratch_shapes=[
             pltpu.VMEM((8, 4, ROWS, WA), BF16),
-            pltpu.VMEM((8, 4, ROWS, WB + EXTRA), BF16),
+            pltpu.VMEM((8, 4, ROWS, WB + EXTRA + WC), BF16),
+            pltpu.VMEM((8, 4, 4, ROWS, WC), BF16),
             pltpu.VMEM((D, 512), BF16),
             pltpu.VMEM((2, PADDED, 1024), BF16),
-            pltpu.VMEM((8, 4, 128, 256), BF16),
+            pltpu.VMEM((8, 4, 2 * SLOTS, 128), BF16),
+            pltpu.VMEM((8, 128, 256), BF16),
             pltpu.VMEM((8, 2, 4, ROWS, PADDED), BF16),
             pltpu.VMEM((8, 2, 2, HALF, PADDED), BF16),
             pltpu.VMEM((8, 2, 2, ROWS, PADDED), BF16),
@@ -512,7 +606,7 @@
             pltpu.VMEM((2, 8, ROWS, PADDED), BF16),
             pltpu.VMEM((8, 128), F32),
             pltpu.VMEM((8, 128), F32),
-            sem((5,)),
+            sem((6,)),
             sem((2,)), sem((2,)),
             sem((4,)), sem((4,)),
             sem((4,)), sem((4,)),
@@ -520,6 +614,7 @@
             sem, sem((8, 4)),
             sem((9,)), sem((9,)),
             sem, sem((8, 4)),
+            sem((4,)), sem((8, 4)),
             sem, sem((8, 4)),
             sem, sem((8, 2)),
             sem, sem((8, 2)),

time: 97.4 us -> 89.9 us (0.923)
  Pallas kernels: 92.7 us -> 85.2 us
    pallas_call x1, Pallas kernels: 92.7 us -> 85.2 us  [per_device(): pl.pallas_call(kernel, out_shape=(jax.ShapeDtypeStruct((ROWS, EIGHTH), BF...]
where the time goes in v4:
time: 89.9 us; the launch traced here: 89 us
  Pallas kernels  85.2 us (95%)
  between operations  2.4 us (3%)
  local copies, waits for them, and re-layouts  1.38 us (2%)
    pallas_call x1, Pallas kernels, per_device(): pl.pallas_call(kernel, out_shape=(jax.ShapeDtypeStruct((ROWS, EIGHTH), BF...  85.2 us

profile of v4, /device:TPU:6, one launch (start us, length us, event | category | flops | bytes accessed | tf_op | source)
XLA Modules:
  0.0 89.0 jit_solution(4102072179480631645)
XLA Ops:
  0.6 85.2 %shard_map.86 = (bf16[32,448]{1,0:T(8,128)(2,1)}, f32[1]{0:T(128)}) custom-call(bf16[32,3584]{1,0:T(8,128)(2,1)} %tokens.1, s32[8,32]{1,0:T(8,128)} %bitcast.4, f32[8,32]{1,0:T(8,128)} %bitcast.5, s32[64]{0:T(128)} %plan.1, bf16[1,3584,128]{2,1,0:T(8,128)(2,1)} %w_gate.1, bf16[1,3584,128]{2,1,0:T(8,128)(2,1)} %w_up.1, bf16[4,2,448,128]{3,2,1,0:T(8,128)(2,1)} %bitcast.3), custom_call_target="tpu_custom_call" | custom-call | flops 6000000000 | bytes 4000000 | tf_op jit(solution)/shard_map/pallas_call | solution.py:582
  85.9 1.4 %copy.11 = bf16[32,448]{1,0:T(8,128)(2,1)} copy(bf16[32,448]{1,0:T(8,128)(2,1)} %get-tuple-element.4) | data formatting | bytes 57344

commit v5 on v4

--- a/solution.py
+++ b/solution.py
@@ -8,7 +8,7 @@
 BF16, F32 = jnp.bfloat16, jnp.float32
 ROWS, HALF = 32, 16
 D = 3584
-WC = 256
+WC = 128
 WA = 1536
 WB = D - WA - 4 * WC
 EXTRA = 128
@@ -190,6 +190,8 @@
         send(ref.at[high], ref.at[high], ax_s.at[3], ax_r.at[3], at_x(-1))
         send_az(1, 0, 2)
         send_az(1, 1, 2)
+        ahead_z(1, 0)
+        ahead_z(1, 1)
         arrived(buf_a.at[zl, xs(3), low], ax_r.at[2])
         arrived(buf_a.at[zl, xs(3), high], ax_r.at[3])
         send_az(1, 0, 3)
@@ -352,14 +354,14 @@
             part[slab, side] = value.astype(BF16).reshape(4, ROWS, PADDED)
         far = part.at[slab, :, xs(3)]
 
-        @pl.when(j < 7)
+        @pl.when(j < 5)
         def _():
             send(far.at[:, low], xin1.at[j, 0], x1_s, x1_r.at[j, 0], at_x(1))
             send(far.at[:, high], xin1.at[j, 1], x1_s, x1_r.at[j, 1], at_x(-1))
 
-        @pl.when(j == 7)
-        def _():
-            send(far, xin3, x1_s, x1_r.at[j, 0], at_x(2))
+        @pl.when(j >= 5)
+        def _():
+            send(far, xin3.at[j - 5], x1_s, x1_r.at[j, 0], at_x(2))
             send(part.at[slab, :, xs(2)], xin2.at[j, 0], x2_s, x2_r.at[j, 0], at_x(1))
             send(part.at[slab, :, xs(1)], xin2.at[j, 1], x2_s, x2_r.at[j, 1], at_x(-1))
 
@@ -414,10 +416,10 @@
             part[slab, :, x].astype(F32) + xin2[j, 0].astype(F32) + xin2[j, 1].astype(F32)
         )
 
-        @pl.when(j == 7)
-        def _():
-            arrived(xin3, x1_r.at[j, 0])
-            xr[slab] = xr[slab] + xin3[...].astype(F32)
+        @pl.when(j >= 5)
+        def _():
+            arrived(xin3.at[j - 5], x1_r.at[j, 0])
+            xr[slab] = xr[slab] + xin3[j - 5].astype(F32)
 
     def send_c(j):
         for k in (1, 2, 3):
@@ -453,8 +455,6 @@
         @pl.when(d == 0)
         def _():
             first_x()
-            ahead_z(1, 0)
-            ahead_z(1, 1)
 
         for q in range(4):
 
@@ -519,7 +519,6 @@
     lax.fori_loop(0, 5, turn, 0)
     experts(4, 0)
     send(cnt, cnt_in, c_s, c_r, peer)
-    pair(3, add_far)
     pair(2, add_near)
     both(2, "on")
     both(6, "alone")
@@ -537,13 +536,6 @@
     copied = plan[ex]
     served = ((r == 0) & (t == ex)) | ((r == 1) & (t == copied))
     load[0] = jnp.sum(jnp.where(served, total, 0.0)) * (1.0 / 256.0)
-
-    mixed = xr[zl, zh]
-    for step in (7, 6, 5, 4):
-        for side in range(2):
-            arrived(zin.at[side, step], z_r.at[side, step])
-            mixed = mixed + zin[side, step].astype(F32)
-    out[...] = mixed[:, 0:EIGHTH].astype(BF16)
 
     block_a, block_b = buf_a.at[0, 0], buf_b.at[0, 0]
     sent(block_a, ax_s.at[0])
@@ -573,6 +565,13 @@
         for step in range(1, 8):
             sent(zout.at[side, step], z_s.at[side, step])
 
+    mixed = xr[zl, zh]
+    for step in (7, 6, 5, 4):
+        for side in range(2):
+            arrived(zin.at[side, step], z_r.at[side, step])
+            mixed = mixed + zin[side, step].astype(F32)
+    out[...] = mixed[:, 0:EIGHTH].astype(BF16)
+
 
 def per_device(tokens, expert_ids, router_gates, replica_plan, w_gate, w_up, w_down):
     hbm = pl.BlockSpec(memory_space=pltpu.HBM)
@@ -600,7 +599,7 @@
             pltpu.VMEM((8, 2, 4, ROWS, PADDED), BF16),
             pltpu.VMEM((8, 2, 2, HALF, PADDED), BF16),
             pltpu.VMEM((8, 2, 2, ROWS, PADDED), BF16),
-            pltpu.VMEM((2, ROWS, PADDED), BF16),
+            pltpu.VMEM((3, 2, ROWS, PADDED), BF16),
             pltpu.VMEM((8, 2, ROWS, PADDED), F32),
             pltpu.VMEM((2, 8, ROWS, PADDED), BF16),
             pltpu.VMEM((2, 8, ROWS, PADDED), BF16),

time: 89.9 us -> 87.6 us (0.974)
  Pallas kernels: 85.2 us -> 83.6 us
    pallas_call x1, Pallas kernels: 85.2 us -> 83.6 us  [per_device(): pl.pallas_call(kernel, out_shape=(jax.ShapeDtypeStruct((ROWS, EIGHTH), BF...]
where the time goes in v5:
time: 87.6 us; the launch traced here: 87.3 us
  Pallas kernels  83.6 us (95%)
  between operations  2.4 us (3%)
  local copies, waits for them, and re-layouts  1.38 us (2%)
    pallas_call x1, Pallas kernels, per_device(): pl.pallas_call(kernel, out_shape=(jax.ShapeDtypeStruct((ROWS, EIGHTH), BF...  83.6 us

profile of v5, /device:TPU:6, one launch (start us, length us, event | category | flops | bytes accessed | tf_op | source)
XLA Modules:
  0.0 87.3 jit_solution(6954884416298099045)
XLA Ops:
  0.6 83.6 %shard_map.86 = (bf16[32,448]{1,0:T(8,128)(2,1)}, f32[1]{0:T(128)}) custom-call(bf16[32,3584]{1,0:T(8,128)(2,1)} %tokens.1, s32[8,32]{1,0:T(8,128)} %bitcast.4, f32[8,32]{1,0:T(8,128)} %bitcast.5, s32[64]{0:T(128)} %plan.1, bf16[1,3584,128]{2,1,0:T(8,128)(2,1)} %w_gate.1, bf16[1,3584,128]{2,1,0:T(8,128)(2,1)} %w_up.1, bf16[4,2,448,128]{3,2,1,0:T(8,128)(2,1)} %bitcast.3), custom_call_target="tpu_custom_call" | custom-call | flops 6000000000 | bytes 4000000 | tf_op jit(solution)/shard_map/pallas_call | solution.py:581
  84.2 1.4 %copy.11 = bf16[32,448]{1,0:T(8,128)(2,1)} copy(bf16[32,448]{1,0:T(8,128)(2,1)} %get-tuple-element.4) | data formatting | bytes 57344

commit v6 on v5

--- a/solution.py
+++ b/solution.py
@@ -9,7 +9,7 @@
 ROWS, HALF = 32, 16
 D = 3584
 WC = 128
-WA = 1536
+WA = 1408
 WB = D - WA - 4 * WC
 EXTRA = 128
 SLOTS = 32

time: 87.6 us -> 89.2 us (1.018)
  Pallas kernels: 83.6 us -> 84.9 us
    pallas_call x1, Pallas kernels: 83.6 us -> 84.9 us  [per_device(): pl.pallas_call(kernel, out_shape=(jax.ShapeDtypeStruct((ROWS, EIGHTH), BF...]
where the time goes in v6:
time: 89.2 us; the launch traced here: 88.7 us
  Pallas kernels  84.9 us (95%)
  between operations  2.4 us (3%)
  local copies, waits for them, and re-layouts  1.38 us (2%)
    pallas_call x1, Pallas kernels, per_device(): pl.pallas_call(kernel, out_shape=(jax.ShapeDtypeStruct((ROWS, EIGHTH), BF...  84.9 us

profile of v6, /device:TPU:6, one launch (start us, length us, event | category | flops | bytes accessed | tf_op | source)
XLA Modules:
  0.0 88.7 jit_solution(14709806931213198873)
XLA Ops:
  0.6 84.9 %shard_map.86 = (bf16[32,448]{1,0:T(8,128)(2,1)}, f32[1]{0:T(128)}) custom-call(bf16[32,3584]{1,0:T(8,128)(2,1)} %tokens.1, s32[8,32]{1,0:T(8,128)} %bitcast.4, f32[8,32]{1,0:T(8,128)} %bitcast.5, s32[64]{0:T(128)} %plan.1, bf16[1,3584,128]{2,1,0:T(8,128)(2,1)} %w_gate.1, bf16[1,3584,128]{2,1,0:T(8,128)(2,1)} %w_up.1, bf16[4,2,448,128]{3,2,1,0:T(8,128)(2,1)} %bitcast.3), custom_call_target="tpu_custom_call" | custom-call | flops 6000000000 | bytes 4000000 | tf_op jit(solution)/shard_map/pallas_call | solution.py:581
  85.5 1.4 %copy.11 = bf16[32,448]{1,0:T(8,128)(2,1)} copy(bf16[32,448]{1,0:T(8,128)(2,1)} %get-tuple-element.4) | data formatting | bytes 57344
